TPU v7x, 128 devices: a whole 4x4x4 slice. The times are simulated.
128 devices in a mesh: gx: 4 (over z), gy: 4 (over y), gz: 8 (over x, core).
Axes of the slice: x: 4, y: 4, z: 4, core: 2. Of those that a mesh axis runs over, the one named last changes fastest.
Arguments:
- rhs: float32 [64, 256, 1024], P('gx', 'gy', 'gz'), may hold values from -8 to 8
- kappa: float32 [64, 256, 1024], P('gx', 'gy', 'gz'), may hold values from 0.09 to 10.1
- sigma: float32 [64, 256, 1024], P('gx', 'gy', 'gz'), may hold values from 0.0005 to 0.01
Outputs:
- correction: float32 [64, 256, 1024], P('gx', 'gy', 'gz')
All inputs are finite; a program needn't handle non-finite values.
Results may differ from a plain program's by a relative error of at most 0.0001.
Values sent between devices are 32-bit elements; how exact they have to be, the bound alone decides.
A program may use at most 256 MiB of HBM per device.

v0:
```python
from functools import partial
import math

import jax
import jax.numpy as jnp
from jax import lax
from jax.sharding import PartitionSpec as P

LEVELS = 4
SWEEPS = 6
BOTTOM_SWEEPS = 8


SHIFTS = ((1, 0, 0), (-1, 0, 0), (0, 1, 0), (0, -1, 0), (0, 0, 1), (0, 0, -1))
MIDDLE_STENCIL = (0, 0, 0)


def with_halo(block, sides, width):
    for axis, dim in sides:
        count = lax.axis_size(axis)
        forward = [(i, i + 1) for i in range(count - 1)]
        backward = [(target, source) for source, target in forward]
        low = lax.ppermute(
            lax.slice_in_dim(block, block.shape[dim] - width, None, axis=dim), axis, forward
        )
        high = lax.ppermute(lax.slice_in_dim(block, 0, width, axis=dim), axis, backward)
        block = jnp.concatenate([low, block, high], axis=dim)
    return block


def cheb(count):
    return [
        1.0 / (1.125 + 0.875 * math.cos(math.pi * (2 * t + 1) / (2 * count))) for t in range(count)
    ]


def slice_window(field, exterior_region, interior_region, stencil_shift):
    return field[
        exterior_region
        - interior_region
        + stencil_shift[0] : field.shape[0]
        - exterior_region
        + interior_region
        + stencil_shift[0],
        exterior_region
        - interior_region
        + stencil_shift[1] : field.shape[1]
        - exterior_region
        + interior_region
        + stencil_shift[1],
        exterior_region
        - interior_region
        + stencil_shift[2] : field.shape[2]
        - exterior_region
        + interior_region
        + stencil_shift[2],
    ]


def apply_stencil_operator(
    value_border, kappa_border, reaction_term, cell_scale, exterior_region, interior_region
):
    middle_point = slice_window(value_border, exterior_region, interior_region, MIDDLE_STENCIL)
    kcentre = slice_window(kappa_border, exterior_region, interior_region, MIDDLE_STENCIL)
    face_flux = jnp.zeros_like(middle_point)
    for stencil_shift in SHIFTS:
        face_weight = 0.5 * (
            kcentre + slice_window(kappa_border, exterior_region, interior_region, stencil_shift)
        )
        face_flux = face_flux + face_weight * (
            middle_point
            - slice_window(value_border, exterior_region, interior_region, stencil_shift)
        )
    return cell_scale * face_flux + reaction_term * middle_point


def diagonal(kappa_border, reaction_term, cell_scale, exterior_region, interior_region):
    kcentre = slice_window(kappa_border, exterior_region, interior_region, MIDDLE_STENCIL)
    weight = jnp.zeros_like(kcentre)
    for stencil_shift in SHIFTS:
        weight = weight + 0.5 * (
            kcentre + slice_window(kappa_border, exterior_region, interior_region, stencil_shift)
        )
    return cell_scale * weight + reaction_term


def restrict(field):
    n0, n1, n2 = field.shape
    return field.reshape(n0 // 2, 2, n1 // 2, 2, n2 // 2, 2).mean(axis=(1, 3, 5))


def prolong(field):
    return jnp.repeat(jnp.repeat(jnp.repeat(field, 2, axis=0), 2, axis=1), 2, axis=2)


def rim(field):
    return with_halo(field, (("gx", 0), ("gy", 1), ("gz", 2)), 1)


def relax(guess, rhs, kappa_border, reaction_term, diag, cell_scale, weights, extend):
    for weight in weights:
        if guess is None:
            guess = weight * rhs / diag
        else:
            image = apply_stencil_operator(
                extend(guess), kappa_border, reaction_term, cell_scale, 1, 0
            )
            guess = guess + weight * (rhs - image) / diag
    return guess


def on_device(rhs, kappa, sigma):
    rhs_now, coef, reaction_term, cell_scale = (rhs, kappa, sigma, 1.0)
    saved = []
    spread_levels = LEVELS
    for level in range(spread_levels):
        kappa_border = with_halo(coef, (("gx", 0), ("gy", 1), ("gz", 2)), 1)
        diag = diagonal(kappa_border, reaction_term, cell_scale, 1, 0)
        smoother = partial(
            relax,
            rhs=rhs_now,
            kappa_border=kappa_border,
            reaction_term=reaction_term,
            diag=diag,
            cell_scale=cell_scale,
            weights=cheb(SWEEPS),
            extend=rim,
        )
        guess = smoother(None)
        residue = rhs_now - apply_stencil_operator(
            rim(guess), kappa_border, reaction_term, cell_scale, 1, 0
        )
        saved.append((guess, smoother))
        rhs_now = restrict(residue)
        coef = restrict(coef)
        reaction_term = restrict(reaction_term)
        cell_scale = cell_scale * 0.25
    kappa_border = with_halo(coef, (("gx", 0), ("gy", 1), ("gz", 2)), 1)
    diag = diagonal(kappa_border, reaction_term, cell_scale, 1, 0)
    result = relax(
        None, rhs_now, kappa_border, reaction_term, diag, cell_scale, cheb(BOTTOM_SWEEPS), rim
    )
    for guess, smoother in reversed(saved):
        result = smoother(guess + prolong(result))
    return result


def solution(mesh):
    placed = (P("gx", "gy", "gz"), P("gx", "gy", "gz"), P("gx", "gy", "gz"))
    return jax.shard_map(
        on_device, mesh=mesh, in_specs=placed, out_specs=P("gx", "gy", "gz"), check_vma=False
    )
```

profile of v0, /device:TPU:1, one launch (start us, length us, event | category | flops | bytes accessed | tf_op | source)
XLA Modules:
  0.0 1669.6 jit_solution(9846930223289638886)
XLA Ops:
  18.4 6.4 collective-permute-start.5
  64.6 4.8 fusion.246
  92.0 5.3 collective-permute-start.17
  122.4 6.6 collective-permute-start.23
  153.9 6.7 collective-permute-start.29
  171.1 34.9 %reshape.116 = f32[8,2,32,2,64,2]{5,4,3,2,1,0:T(8,128)} reshape(f32[16,64,128]{2,1,0:T(8,128)S(1)} %copy-done) | data formatting | bytes 1048576 | tf_op jit(solution)/shard_map/reshape | solution.py:89
  206.0 12.2 reduce_sum.130
  232.2 5.5 collective-permute-start.35
  245.8 34.9 %reshape.117 = f32[8,2,32,2,64,2]{5,4,3,2,1,0:T(8,128)} reshape(f32[16,64,128]{2,1,0:T(8,128)S(1)} %copy-done.1) | data formatting | bytes 1048576 | tf_op jit(solution)/shard_map/reshape | solution.py:89
  280.7 12.2 reduce_sum.131
  323.3 6.5 collective-permute-start.41
  342.9 4.6 fusion.136
  347.5 35.7 %reshape.115 = f32[8,2,32,2,64,2]{5,4,3,2,1,0:T(8,128)} reshape(f32[16,64,128]{2,1,0:T(8,128)} %fusion.136) | data formatting | bytes 1048576 | tf_op jit(solution)/shard_map/reshape | solution.py:89
  383.2 12.2 reduce_sum.129
  415.2 4.8 collective-permute-start.53
  437.3 7.2 collective-permute-start.59
  461.8 7.2 collective-permute-start.65
  486.9 7.2 collective-permute-start.71
  494.2 5.7 div.233
  513.7 4.6 collective-permute-start.85
  521.1 4.7 collective-permute-start.77
  525.9 5.7 div.235
  564.8 5.7 reshape.118
  614.5 6.6 collective-permute-start.101
  636.7 7.1 collective-permute-start.107
  660.1 7.1 collective-permute-start.113
  682.4 4.6 collective-permute-start.127
  689.7 5.5 collective-permute-start.119
  772.6 5.7 collective-permute-start.143
  793.4 7.1 collective-permute-start.149
  818.5 7.1 collective-permute-start.155
  832.2 4.6 collective-permute-start.157
  852.7 5.2 collective-permute-start.161
  908.6 5.5 collective-permute-start.179
  929.7 7.1 collective-permute-start.185
  952.3 7.1 collective-permute-start.191
  974.9 7.1 collective-permute-start.197
  997.5 7.1 collective-permute-start.203
  1020.1 7.1 collective-permute-start.209
  1042.7 7.1 collective-permute-start.215
  1070.6 7.1 collective-permute-start.221
  1093.5 7.1 collective-permute-start.227
  1116.4 7.1 collective-permute-start.233
  1139.3 7.1 collective-permute-start.239
  1162.2 7.1 collective-permute-start.245
  1185.1 7.1 collective-permute-start.251
  1211.9 7.3 collective-permute-start.257
  1234.8 7.1 collective-permute-start.263
  1257.5 7.1 collective-permute-start.269
  1280.2 7.1 collective-permute-start.275
  1303.0 7.1 collective-permute-start.281
  1325.7 7.1 collective-permute-start.287
  1352.1 7.1 collective-permute-start.293
  1376.5 7.2 collective-permute-start.299
  1400.9 7.2 collective-permute-start.305
  1425.4 7.2 collective-permute-start.311
  1449.9 7.2 collective-permute-start.317
  1474.4 7.2 collective-permute-start.323
  1506.5 7.3 collective-permute-start.329
  1536.9 7.1 collective-permute-start.335
  1567.0 7.1 collective-permute-start.341
  1597.2 7.1 collective-permute-start.347
  1626.7 6.7 collective-permute-start.353
  1657.0 6.7 collective-permute-start.359
  (1149 shorter events, 1143.1 us)
Async XLA Ops:
  87.4 10.0 collective-permute-start.16
  119.0 10.0 collective-permute-start.22
  150.7 10.0 collective-permute-start.28
  168.0 50.3 %collective-permute-start.31 = (f32[1,64,128]{2,1,0:T(8,128)S(1)}, f32[1,64,128]{2,1,0:T(8,128)S(1)}, u32[]{:S(2)}, u32[]{:S(2)}) collective-permute-start(f32[1,64,128]{2,1,0:T(8,128)S(1)} %get-tuple-element.102), channel_id=1, source_target_pairs={{0,32},{32,64},{64,96},{1,33},{33,65},{65,97},{2,34},{34,66},{66,9... | collective-permute-start | bytes 98312 | tf_op jit(solution)/shard_map/ppermute | solution.py:23
  169.6 48.7 %collective-permute-start.30 = (f32[1,64,128]{2,1,0:T(8,128)S(1)}, f32[1,64,128]{2,1,0:T(8,128)S(1)}, u32[]{:S(2)}, u32[]{:S(2)}) collective-permute-start(f32[1,64,128]{2,1,0:T(8,128)S(1)} %get-tuple-element.103), channel_id=1, source_target_pairs={{32,0},{64,32},{96,64},{33,1},{65,33},{97,65},{34,2},{66,34},{98,6... | collective-permute-start | bytes 98312 | tf_op jit(solution)/shard_map/ppermute | solution.py:26
  232.2 62.7 %collective-permute-start.35 = (f32[18,66,1]{1,2,0:T(1,128)}, f32[18,66,1]{1,2,0:T(1,128)}, u32[]{:S(2)}, u32[]{:S(2)}) collective-permute-start(f32[18,66,1]{1,2,0:T(1,128)} %copy.578), channel_id=1, source_target_pairs={{0,1},{1,2},{2,3},{3,4},{4,5},{5,6},{6,7},{8,9},{9,10},{10,11},{11... | collective-permute-start | bytes 14264 | tf_op jit(solution)/shard_map/ppermute | solution.py:23
  237.7 55.2 %collective-permute-start.34 = (f32[18,66,1]{1,2,0:T(1,128)}, f32[18,66,1]{1,2,0:T(1,128)}, u32[]{:S(2)}, u32[]{:S(2)}) collective-permute-start(f32[18,66,1]{1,2,0:T(1,128)} %copy.577), channel_id=1, source_target_pairs={{1,0},{2,1},{3,2},{4,3},{5,4},{6,5},{7,6},{9,8},{10,9},{11,10},{12... | collective-permute-start | bytes 14264 | tf_op jit(solution)/shard_map/ppermute | solution.py:26
  240.2 65.8 %collective-permute-start.43 = (f32[1,32,64]{2,1,0:T(8,128)}, f32[1,32,64]{2,1,0:T(8,128)S(1)}, u32[]{:S(2)}, u32[]{:S(2)}) collective-permute-start(f32[1,32,64]{2,1,0:T(8,128)} %get-tuple-element.190), channel_id=1, source_target_pairs={{0,32},{32,64},{64,96},{1,33},{33,65},{65,97},{2,34},{34,66},{66,9... | collective-permute-start | bytes 24584 | tf_op jit(solution)/shard_map/ppermute | solution.py:23
  244.5 61.5 %collective-permute-start.42 = (f32[1,32,64]{2,1,0:T(8,128)}, f32[1,32,64]{2,1,0:T(8,128)S(1)}, u32[]{:S(2)}, u32[]{:S(2)}) collective-permute-start(f32[1,32,64]{2,1,0:T(8,128)} %get-tuple-element.191), channel_id=1, source_target_pairs={{32,0},{64,32},{96,64},{33,1},{65,33},{97,65},{34,2},{66,34},{98,6... | collective-permute-start | bytes 24584 | tf_op jit(solution)/shard_map/ppermute | solution.py:26
  323.3 17.8 %collective-permute-start.41 = (f32[18,66,1]{1,2,0:T(1,128)}, f32[18,66,1]{1,2,0:T(1,128)}, u32[]{:S(2)}, u32[]{:S(2)}) collective-permute-start(f32[18,66,1]{1,2,0:T(1,128)} %copy.580), channel_id=1, source_target_pairs={{0,1},{1,2},{2,3},{3,4},{4,5},{5,6},{6,7},{8,9},{9,10},{10,11},{11... | collective-permute-start | bytes 14264 | tf_op jit(solution)/shard_map/ppermute | solution.py:23
  329.8 9.3 collective-permute-start.40
  333.6 61.9 %collective-permute-start.47 = (f32[10,34,1]{2,1,0:T(8,128)}, f32[10,34,1]{2,1,0:T(8,128)}, u32[]{:S(2)}, u32[]{:S(2)}) collective-permute-start(f32[10,34,1]{2,1,0:T(8,128)} %get-tuple-element.138), channel_id=1, source_target_pairs={{0,1},{1,2},{2,3},{3,4},{4,5},{5,6},{6,7},{8,9},{9,10},{10,11},{11... | collective-permute-start | bytes 4088 | tf_op jit(solution)/shard_map/ppermute | solution.py:23
  337.2 58.2 %collective-permute-start.46 = (f32[10,34,1]{2,1,0:T(8,128)}, f32[10,34,1]{2,1,0:T(8,128)}, u32[]{:S(2)}, u32[]{:S(2)}) collective-permute-start(f32[10,34,1]{2,1,0:T(8,128)} %get-tuple-element.139), channel_id=1, source_target_pairs={{1,0},{2,1},{3,2},{4,3},{5,4},{6,5},{7,6},{9,8},{10,9},{11,10},{12... | collective-permute-start | bytes 4088 | tf_op jit(solution)/shard_map/ppermute | solution.py:26
  411.6 9.9 collective-permute-start.52
  435.4 10.7 collective-permute-start.58
  437.3 9.9 collective-permute-start.59
  459.9 10.7 collective-permute-start.64
  461.8 9.9 collective-permute-start.65
  485.0 17.4 %collective-permute-start.70 = (f32[10,34,1]{2,1,0:T(8,128)}, f32[10,34,1]{2,1,0:T(8,128)S(1)}, u32[]{:S(2)}, u32[]{:S(2)}) collective-permute-start(f32[10,34,1]{2,1,0:T(8,128)} %get-tuple-element.130), channel_id=1, source_target_pairs={{1,0},{2,1},{3,2},{4,3},{5,4},{6,5},{7,6},{9,8},{10,9},{11,10},{12... | collective-permute-start | bytes 4088 | tf_op jit(solution)/shard_map/ppermute | solution.py:26
  486.9 15.5 collective-permute-start.71
  508.9 9.4 collective-permute-start.75
  512.5 25.7 %collective-permute-start.84 = (f32[1,16,32]{2,1,0:T(8,128)}, f32[1,16,32]{2,1,0:T(8,128)}, u32[]{:S(2)}, u32[]{:S(2)}) collective-permute-start(f32[1,16,32]{2,1,0:T(8,128)} %get-tuple-element.294), channel_id=1, source_target_pairs={{32,0},{64,32},{96,64},{33,1},{65,33},{97,65},{34,2},{66,34},{98,6... | collective-permute-start | bytes 6152 | tf_op jit(solution)/shard_map/ppermute | solution.py:26
  513.7 24.4 %collective-permute-start.85 = (f32[1,16,32]{2,1,0:T(8,128)}, f32[1,16,32]{2,1,0:T(8,128)}, u32[]{:S(2)}, u32[]{:S(2)}) collective-permute-start(f32[1,16,32]{2,1,0:T(8,128)} %get-tuple-element.295), channel_id=1, source_target_pairs={{0,32},{32,64},{64,96},{1,33},{33,65},{65,97},{2,34},{34,66},{66,9... | collective-permute-start | bytes 6152 | tf_op jit(solution)/shard_map/ppermute | solution.py:23
  519.2 15.0 collective-permute-start.76
  521.1 13.1 collective-permute-start.77
  538.9 10.9 collective-permute-start.87
  553.1 11.4 collective-permute-start.82
  560.2 12.8 collective-permute-start.89
  562.6 11.1 collective-permute-start.88
  658.2 12.0 collective-permute-start.112
  660.1 10.1 collective-permute-start.113
  677.6 9.4 collective-permute-start.117
  681.1 21.4 %collective-permute-start.126 = (f32[1,8,16]{2,1,0:T(8,128)}, f32[1,8,16]{2,1,0:T(8,128)}, u32[]{:S(2)}, u32[]{:S(2)}) collective-permute-start(f32[1,8,16]{2,1,0:T(8,128)} %get-tuple-element.364), channel_id=1, source_target_pairs={{32,0},{64,32},{96,64},{33,1},{65,33},{97,65},{34,2},{66,34},{98,6... | collective-permute-start | bytes 1544 | tf_op jit(solution)/shard_map/ppermute | solution.py:26
  682.4 20.1 %collective-permute-start.127 = (f32[1,8,16]{2,1,0:T(8,128)}, f32[1,8,16]{2,1,0:T(8,128)}, u32[]{:S(2)}, u32[]{:S(2)}) collective-permute-start(f32[1,8,16]{2,1,0:T(8,128)} %get-tuple-element.365), channel_id=1, source_target_pairs={{0,32},{32,64},{64,96},{1,33},{33,65},{65,97},{2,34},{34,66},{66,9... | collective-permute-start | bytes 1544 | tf_op jit(solution)/shard_map/ppermute | solution.py:23
  687.7 11.1 collective-permute-start.118
  703.3 10.9 collective-permute-start.129
  717.4 12.0 collective-permute-start.124
  719.3 10.1 collective-permute-start.125
  816.6 13.3 collective-permute-start.154
  818.5 11.4 collective-permute-start.155
  825.6 19.6 %collective-permute-start.169 = (f32[1,4,8]{2,1,0:T(4,128)}, f32[1,4,8]{2,1,0:T(4,128)}, u32[]{:S(2)}, u32[]{:S(2)}) collective-permute-start(f32[1,4,8]{2,1,0:T(4,128)} %multiply_bitcast_fusion), channel_id=1, source_target_pairs={{0,32},{32,64},{64,96},{1,33},{33,65},{65,97},{2,34},{34,66},{66,9... | collective-permute-start | bytes 392 | tf_op jit(solution)/shard_map/ppermute | solution.py:23
  828.7 16.5 collective-permute-start.168
  832.2 9.3 collective-permute-start.157
  846.0 18.8 %collective-permute-start.171 = (f32[3,1,8]{2,1,0:T(1,128)S(1)}, f32[3,1,8]{2,1,0:T(1,128)S(1)}, u32[]{:S(2)}, u32[]{:S(2)}) collective-permute-start(f32[3,1,8]{2,1,0:T(1,128)S(1)} %get-tuple-element.380), channel_id=1, source_target_pairs={{0,8},{8,16},{16,24},{1,9},{9,17},{17,25},{2,10},{10,18},{18,26},{... | collective-permute-start | bytes 296 | tf_op jit(solution)/shard_map/ppermute | solution.py:23
  867.8 10.4 collective-permute-start.165
  873.8 16.2 collective-permute-start.173
  1209.9 9.2 collective-permute-start.256
  1350.2 10.6 collective-permute-start.292
  1352.1 9.8 collective-permute-start.293
  1374.5 10.7 collective-permute-start.298
  1376.5 9.9 collective-permute-start.299
  1399.0 10.7 collective-permute-start.304
  1400.9 9.9 collective-permute-start.305
  1423.5 10.7 collective-permute-start.310
  1425.4 9.9 collective-permute-start.311
  1448.0 10.7 collective-permute-start.316
  1449.9 9.9 collective-permute-start.317
  1472.5 10.7 collective-permute-start.322
  1474.4 9.9 collective-permute-start.323
  1503.2 10.6 collective-permute-start.328
  1533.6 10.4 collective-permute-start.334
  1563.7 10.4 collective-permute-start.340
  1593.9 10.4 collective-permute-start.346
  1653.7 10.0 collective-permute-start.358
  (341 other events, 4305.6 us)
where the time goes:
time: 1690 us; the launch traced here: 1670 us
  starting transfers between devices  910 us (54%)
  waiting for transfers between devices  365 us (22%)
  local copies, waits for them, and re-layouts  244 us (14%)
  other arithmetic  144 us (9%)
    ppermute x180, starting transfers between devices, with_halo(): lax.ppermute(lax.slice_in_dim(block, block.shape[dim] - width, None, axis...  627 us
    ppermute x180, waiting for transfers between devices, with_halo(): lax.ppermute(lax.slice_in_dim(block, 0, width, axis=dim), axis, backward)  327 us
    ppermute x180, starting transfers between devices, with_halo(): lax.ppermute(lax.slice_in_dim(block, 0, width, axis=dim), axis, backward)  283 us
    reshape x5, local copies, waits for them, and re-layouts, restrict(): field.reshape(n0 // 2, 2, n1 // 2, 2, n2 // 2, 2).mean(axis=(1, 3, 5))  112 us
    add x51, other arithmetic, relax(): guess = guess + weight * (rhs - image) / diag  58.2 us
    reduce_sum x15, other arithmetic, restrict(): field.reshape(n0 // 2, 2, n1 // 2, 2, n2 // 2, 2).mean(axis=(1, 3, 5))  56 us
    ppermute x180, waiting for transfers between devices, with_halo(): lax.ppermute(lax.slice_in_dim(block, block.shape[dim] - width, None, axis...  38.9 us
    unnamed x118, local copies, waits for them, and re-layouts  38.7 us
  transfers between devices with their start and end apart: 360, of which 161 were waited for; matrix products, arithmetic and copies ran while one was open for 15% of the time, Pallas kernels for 0%

commit v1 on v0

v1 whole, which is shorter than its diff:
```python
from functools import partial
import math

import jax
import jax.numpy as jnp
from jax import lax
from jax.experimental import pallas as pl
from jax.experimental.pallas import tpu as pltpu
from jax.sharding import PartitionSpec as P

LEVELS = 4
SWEEPS = 6
BOTTOM_SWEEPS = 8
MESH = pl.DeviceIdType.MESH
F32 = jnp.float32
COPIES = 256


def cheb(count):
    return [
        1.0 / (1.125 + 0.875 * math.cos(math.pi * (2 * t + 1) / (2 * count))) for t in range(count)
    ]


def lane(rows):
    return lax.broadcasted_iota(jnp.int32, (rows, 128), 1)


def turn(value, shift):
    shift = shift % 128
    return value if shift == 0 else pltpu.roll(value, shift, 1)


def product(value, matrix):
    return jnp.dot(value, matrix, precision=lax.Precision.HIGHEST, preferred_element_type=F32)


def halving(fine0, coarse0, count):
    i = lax.broadcasted_iota(jnp.int32, (128, 128), 0)
    j = lax.broadcasted_iota(jnp.int32, (128, 128), 1)
    offset = (i - fine0) - 2 * (j - coarse0)
    good = ((offset == 0) | (offset == 1)) & (j >= coarse0) & (j < coarse0 + count)
    return jnp.where(good, 0.125, 0.0).astype(F32)


def doubling(coarse0, fine0, low, high):
    i = lax.broadcasted_iota(jnp.int32, (128, 128), 0)
    j = lax.broadcasted_iota(jnp.int32, (128, 128), 1)
    offset = (j - fine0) - 2 * (i - coarse0)
    good = ((offset == 0) | (offset == 1)) & (j >= low) & (j < high)
    return jnp.where(good, 1.0, 0.0).astype(F32)


class Links:
    def __init__(self, send, recv):
        self.send, self.recv, self.used = send, recv, 0

    def copy(self, src, dst, target, send_ok=None, recv_ok=None):
        k = self.used
        self.used += 1
        made = pltpu.make_async_remote_copy(
            src_ref=src,
            dst_ref=dst,
            send_sem=self.send.at[k],
            recv_sem=self.recv.at[k],
            device_id=target,
            device_id_type=MESH,
        )
        return made, send_ok, recv_ok


def given(flag, action):
    if flag is None:
        action()
    else:
        pl.when(flag)(action)


def start(copies):
    for made, send_ok, _ in copies:
        given(send_ok, made.start)


def wait(copies):
    for made, _, recv_ok in copies:
        given(recv_ok, made.wait_recv)
    for made, send_ok, _ in copies:
        given(send_ok, made.wait_send)


def both(a, b):
    if a is None:
        return b
    return a if b is None else a & b


class Level:
    def __init__(self, tiles, row0, rows, scale, closed=False):
        self.tiles, self.row0, self.rows, self.scale, self.closed = tiles, row0, rows, scale, closed

    def window(self, shift=0):
        return pl.ds(self.row0 + shift, self.rows)

    def beside(self, values):
        n = lane(self.rows)
        left = [turn(v, 1) for v in values]
        right = [turn(v, -1) for v in values]
        if self.tiles == 2:
            left = [jnp.where(n == 0, left[1 - t], left[t]) for t in range(2)]
            right = [jnp.where(n == 127, right[1 - t], right[t]) for t in range(2)]
        return left, right

    def near(self, ref, p, tiles):
        mid = [ref[t, p, self.window(), :] for t in range(self.tiles)]
        left, right = self.beside(mid)
        return mid, [
            (
                ref[t, p + 1, self.window(), :],
                ref[t, p - 1, self.window(), :],
                ref[t, p, self.window(1), :],
                ref[t, p, self.window(-1), :],
                left[t],
                right[t],
            )
            for t in range(tiles)
        ]

    def coefficients(self, kappa, sigma, coef, low, high, finish):
        n = lane(self.rows)

        def body(p, carry):
            mid, around = self.near(kappa, p, self.tiles)
            for t in range(self.tiles):
                k, near = mid[t], list(around[t])
                if self.closed:
                    near[4] = jnp.where(n == 0, 0.0, near[4])
                    near[5] = jnp.where(n == 127, 0.0, near[5])
                face = [(0.5 * self.scale) * (k + j) for j in near]
                diag = face[0] + face[1] + face[2] + face[3] + face[4] + face[5]
                diag = diag + sigma[t, p, self.window(), :]
                inverse = jnp.where(k > 0.0, 1.0 / diag, 0.0)
                if self.closed:
                    face[4] = jnp.where(n == 0, 0.0, face[4])
                    face[5] = jnp.where(n == 127, 0.0, face[5])
                for j in range(6):
                    coef[j, t, p, self.window(), :] = face[j] * inverse
                finish(t, p, diag, inverse)
            return carry

        lax.fori_loop(low, high, body, 0)

    def defect(self, x, rhs, coef, p, tiles):
        mid, around = self.near(x, p, tiles)
        out = []
        for t in range(tiles):
            total = rhs[t, p, self.window(), :] - mid[t]
            for j in range(6):
                total = total + coef[j, t, p, self.window(), :] * around[t][j]
            out.append(total)
        return mid, out

    def sweep(self, src, dst, rhs, coef, weight, low, high):
        def body(p, carry):
            mid, out = self.defect(src, rhs, coef, p, self.tiles)
            for t in range(self.tiles):
                dst[t, p, self.window(), :] = mid[t] + weight * out[t]
            return carry

        lax.fori_loop(low, high, body, 0)

    def residual(self, x, rhs, coef, diag, dst, low, high):
        def body(p, carry):
            _, out = self.defect(x, rhs, coef, p, 1)
            dst[0, p, self.window(), :] = diag[0, p, self.window(), :] * out[0]
            return carry

        lax.fori_loop(low, high, body, 0)


def restrict(load, planes, matrix, store):
    sums = [
        load(2 * i, 0) + load(2 * i, 1) + load(2 * i + 1, 0) + load(2 * i + 1, 1)
        for i in range(planes)
    ]
    rows = sums[0].shape[0]
    out = product(jnp.concatenate(sums, axis=0), matrix)
    for i in range(planes):
        store(i, out[i * rows : (i + 1) * rows, :])


def kernel(rhs, kappa, sigma, out, s):
    gx, gy, gz = lax.axis_index("gx"), lax.axis_index("gy"), lax.axis_index("gz")
    nx, ny, nz = 4, 4, 8
    links = Links(s["send"], s["recv"])
    has = {
        ("x", 1): gx < nx - 1,
        ("x", -1): gx > 0,
        ("y", 1): gy < ny - 1,
        ("y", -1): gy > 0,
        ("z", 1): gz < nz - 1,
        ("z", -1): gz > 0,
        ("x", 0): None,
        ("y", 0): None,
    }

    def clear(ref, *index):
        part = ref.at[index] if index else ref
        part[...] = jnp.zeros(part.shape, F32)

    def clear_edges(ref, planes, rows):
        total = ref.shape[1]
        pl.when(gx == 0)(lambda: clear(ref, 0, pl.ds(0, planes[0])))
        pl.when(gx == nx - 1)(lambda: clear(ref, 0, pl.ds(planes[1], total - planes[1])))
        pl.when(gy == 0)(lambda: clear(ref, 0, slice(None), pl.ds(rows[0], rows[1])))
        pl.when(gy == ny - 1)(lambda: clear(ref, 0, slice(None), pl.ds(rows[2], rows[1])))

    for name in ("K0", "S0", "B0", "N0"):
        clear_edges(s[name], (7, 23), (8, 8, 80))
    for name in ("K1", "S1", "B1", "N1", "E1"):
        clear_edges(s[name], (8, 16), (8, 8, 48))
    for name in ("K2", "S2", "B2", "N2"):
        pl.when(gy == 0)(lambda ref=s[name]: clear(ref, 0, slice(None), pl.ds(8, 16)))
        pl.when(gy == ny - 1)(lambda ref=s[name]: clear(ref, 0, slice(None), pl.ds(40, 16)))
    for name in ("K2", "XA2", "XB2"):
        clear(s[name], 0, 0)
        clear(s[name], 0, 17)
    for name, planes, rows in (("3", 8, 32), ("4", 4, 16)):
        for field in ("K", "XA", "XB"):
            ref = s[field + name]
            clear(ref, 0, 0)
            clear(ref, 0, planes + 1)
            clear(ref, 0, slice(None), pl.ds(0, 8))
            clear(ref, 0, slice(None), pl.ds(8 + rows, 8))
    for name in ("G0", "GN0"):
        clear(s[name])

    @pl.when((gz == 0) | (gz == nz - 1))
    def _():
        for name in ("Z0", "ZN0", "Z1", "Z2"):
            clear(s[name])

    barrier = pltpu.get_barrier_semaphore()
    plane_mates = [
        (lax.rem(gx + i, nx), lax.rem(gy + j, ny), gz)
        for i in range(nx)
        for j in range(ny)
        if i or j
    ]
    line_mates = [(gx, gy, lax.rem(gz + i, nz)) for i in range(1, nz)]
    for mate in plane_mates + line_mates:
        pl.semaphore_signal(barrier, inc=1, device_id=mate, device_id_type=MESH)
    pl.semaphore_wait(barrier, len(plane_mates + line_mates))

    around = [(dx, dy) for dx in (1, -1, 0) for dy in (0, 1, -1) if dx or dy]

    def neighbours(make):
        copies = []
        for dx, dy in around:
            src, dst = make(dx, dy)
            copies.append(
                links.copy(
                    src,
                    dst,
                    (gx + dx, gy + dy, gz),
                    both(has["x", dx], has["y", dy]),
                    both(has["x", -dx], has["y", -dy]),
                )
            )
        return copies

    def sides(src, slots):
        return [
            links.copy(src, slots.at[0], (gx, gy, gz + 1), has["z", 1], has["z", -1]),
            links.copy(src, slots.at[1], (gx, gy, gz - 1), has["z", -1], has["z", 1]),
        ]

    def main0(src, first, ref, h):
        def make(dx, dy):
            sp = {1: (first + 16 - h, h), -1: (first, h), 0: (first, 16)}[dx]
            dp = {1: (7 - h, h), -1: (23, h), 0: (7, 16)}[dx]
            sr = {1: (56, 8), -1: (0, 8), 0: (0, 64)}[dy]
            dr = {1: (8, 8), -1: (80, 8), 0: (16, 64)}[dy]
            base = 0 if src is not ref else 16
            source = src.at[pl.ds(*sp), pl.ds(base + sr[0], sr[1])] if base == 0 else src.at[
                0, pl.ds(*sp), pl.ds(base + sr[0], sr[1])
            ]
            return source, ref.at[0, pl.ds(*dp), pl.ds(*dr)]

        return neighbours(make)

    inner = [
        pltpu.make_async_copy(src, s[name].at[0, pl.ds(7, 16), pl.ds(16, 64)], s["local"].at[k])
        for k, (src, name) in enumerate(((kappa, "K0"), (sigma, "S0"), (rhs, "B0")))
    ]
    for made in inner:
        made.start()
    mains = main0(kappa, 0, s["K0"], 7) + main0(sigma, 0, s["S0"], 6) + main0(rhs, 0, s["B0"], 6)
    start(mains)
    for made in inner:
        made.wait()

    def pack0(load, dst):
        n = lane(64)
        for g in range(2):
            total = jnp.zeros((64, 128), F32)
            for q in range(8):
                moved = turn(load(8 * g + q), 16 * q + 8)
                total = jnp.where((n >= 16 * q) & (n < 16 * q + 16), moved, total)
            dst[g, :, :] = total

    for a, name in enumerate(("K0", "S0", "B0")):
        pack0(lambda i, ref=s[name]: ref[0, 7 + i, 16:80, :], s["P0"].at[a])
    side0 = sides(s["P0"], s["Z0"])
    start(side0)

    to1 = halving(0, 32, 64)
    to2 = halving(32, 48, 32)
    to3 = halving(48, 16 * gz, 16)
    to4 = halving(0, 0, 64)
    own2 = pl.ds(1 + 4 * gx, 4)
    own3 = pl.ds(1 + 2 * gx, 2)
    row3 = pl.ds(pl.multiple_of(8 + 8 * gy, 8), 8)

    def down1(src, first, row, dst):
        def store(i, v):
            dst[0, 8 + i, 16:48, :] = v

        restrict(lambda i, o: src[0, first + i, pl.ds(row + o, 32, stride=2), :], 8, to1, store)

    def down2(src, dst):
        def store(i, v):
            dst[0, 1 + 4 * gx + i, 24:40, :] = v

        restrict(lambda i, o: src[0, 8 + i, pl.ds(16 + o, 16, stride=2), :], 4, to2, store)

    def down3(src, use):
        def store(i, v):
            s["Z3"][use, gz, i, :, :] = v

        restrict(
            lambda i, o: src[0, 1 + 4 * gx + i, pl.ds(24 + o, 8, stride=2), :], 2, to3, store
        )

    def down4(src, dst):
        def store(i, v):
            dst[0, 1 + i, 8:24, :] = v

        restrict(lambda i, o: src[0, 1 + i, pl.ds(8 + o, 16, stride=2), :], 4, to4, store)

    def side1(ref, use):
        n = lane(32)
        total = jnp.zeros((32, 128), F32)
        for q in range(8):
            v = ref[0, 8 + q, 16:48, :]
            v = turn(v + turn(v, 64), 16 * q - 24)
            total = jnp.where((n >= 16 * q) & (n < 16 * q + 16), v, total)
        s["P1"][use, :, :] = total
        return sides(s["P1"].at[use], s["Z1"].at[use])

    def merge1(ref, use):
        n = lane(32)
        ghosts = jnp.where((n % 16) < 8, s["Z1"][use, 0], s["Z1"][use, 1])
        for q in range(8):
            low = turn(ghosts, 24 - 16 * q)
            high = turn(ghosts, 24 - 16 * q + 64)
            v = ref[0, 8 + q, 16:48, :]
            v = jnp.where((n >= 24) & (n < 32), low, v)
            ref[0, 8 + q, 16:48, :] = jnp.where((n >= 96) & (n < 104), high, v)

    def main1(ref, h):
        def make(dx, dy):
            sp = {1: (16 - h, h), -1: (8, h), 0: (8, 8)}[dx]
            dp = {1: (8 - h, h), -1: (16, h), 0: (8, 8)}[dx]
            sr = {1: (40, 8), -1: (16, 8), 0: (16, 32)}[dy]
            dr = {1: (8, 8), -1: (48, 8), 0: (16, 32)}[dy]
            return ref.at[0, pl.ds(*sp), pl.ds(*sr)], ref.at[0, pl.ds(*dp), pl.ds(*dr)]

        return neighbours(make)

    def side2(ref, use):
        return sides(ref.at[0, own2, pl.ds(24, 16)], s["Z2"].at[use])

    def merge2(ref, use):
        for i in range(4):
            p = 1 + 4 * gx + i
            ref[0, p, 24:40, :] = (
                ref[0, p, 24:40, :]
                + turn(s["Z2"][use, 0, i], -32)
                + turn(s["Z2"][use, 1, i], 32)
            )

    def main2(ref):
        copies = []
        for i in range(nx):
            for dy in (0, 1, -1):
                if i == 0 and dy == 0:
                    continue
                dr = {1: (8, 16), -1: (40, 16), 0: (24, 16)}[dy]
                copies.append(
                    links.copy(
                        ref.at[0, own2, pl.ds(24, 16)],
                        ref.at[0, own2, pl.ds(*dr)],
                        (lax.rem(gx + i, nx), gy + dy, gz),
                        has["y", dy],
                        has["y", -dy],
                    )
                )
        return copies

    def side3(use):
        part = s["Z3"].at[use, gz]
        return [links.copy(part, part, mate) for mate in line_mates]

    def merge3(ref, use):
        for i in range(2):
            total = s["Z3"][use, 0, i]
            for q in range(1, nz):
                total = total + s["Z3"][use, q, i]
            ref[0, 1 + 2 * gx + i, row3, :] = total

    def main3(ref):
        part = ref.at[0, own3, row3]
        return [links.copy(part, part, mate) for mate in plane_mates]

    down1(s["K0"], 7, 16, s["K1"])
    down1(s["S0"], 7, 16, s["S1"])
    sent = side1(s["K1"], 0) + side1(s["S1"], 1)
    start(sent)
    down2(s["K1"], s["K2"])
    down2(s["S1"], s["S2"])
    more = side2(s["K2"], 0) + side2(s["S2"], 1)
    start(more)
    sent = sent + more
    down3(s["K2"], 0)
    down3(s["S2"], 1)
    more = side3(0) + side3(1)
    start(more)
    sent = sent + more

    wait(side0)
    n64 = lane(64)
    for a in range(3):
        for g in range(2):
            s["G0"][a, 1 + g, 8:72, :] = jnp.where(
                (n64 % 16) < 8, s["Z0"][0, a, g], s["Z0"][1, a, g]
            )

    def ghost0(ref):
        def make(dx, dy):
            sg = {1: (2, 1), -1: (1, 1), 0: (1, 2)}[dx]
            dg = {1: (0, 1), -1: (3, 1), 0: (1, 2)}[dx]
            sr = {1: (64, 8), -1: (8, 8), 0: (8, 64)}[dy]
            dr = {1: (0, 8), -1: (72, 8), 0: (8, 64)}[dy]
            every = slice(None)
            return ref.at[every, pl.ds(*sg), pl.ds(*sr)], ref.at[every, pl.ds(*dg), pl.ds(*dr)]

        return neighbours(make)

    def unpack0(src, ref):
        n = lane(80)
        edge = (n < 8) | (n >= 120)

        for g in range(4):
            v = src[g]
            for q in range(8):
                p = 8 * g + q - 1
                if 0 <= p < 30:
                    ref[1, p, 8:88, :] = jnp.where(edge, turn(v, -16 * q - 8), 0.0)

    ghosts = ghost0(s["G0"])
    start(ghosts)

    wait(sent)
    merge1(s["K1"], 0)
    merge1(s["S1"], 1)
    merge2(s["K2"], 0)
    merge2(s["S2"], 1)
    merge3(s["K3"], 0)
    merge3(s["S3"], 1)
    coarse = main1(s["K1"], 7) + main1(s["S1"], 7) + main2(s["K2"]) + main2(s["S2"])
    coarse = coarse + main3(s["K3"]) + main3(s["S3"])
    start(coarse)

    wait(ghosts)
    for a, name in enumerate(("K0", "S0", "B0")):
        unpack0(s["G0"].at[a], s[name])
    wait(mains)

    weights = cheb(SWEEPS)
    level0 = Level(2, 8, 80, 1.0)
    c0, b0, xa0, xb0 = s["C0"], s["B0"], s["S0"], s["XB0"]

    def finish0(t, p, diag, inverse):
        scaled = b0[t, p, 8:88, :] * inverse
        b0[t, p, 8:88, :] = scaled
        xa0[t, p, 8:88, :] = weights[0] * scaled
        if t == 0:
            s["D0"][0, p, :, :] = diag[8:72, :]

    level0.coefficients(s["K0"], s["S0"], c0, 1, 29, finish0)
    x, y = xa0, xb0
    for t in range(1, SWEEPS):
        level0.sweep(x, y, b0, c0, weights[t], 7 - (6 - t), 23 + (6 - t))
        x, y = y, x

    inside0 = Level(2, 16, 64, 1.0)

    def residual0(p, carry):
        _, defect = inside0.defect(x, b0, c0, p, 1)
        s["R0"][0, p, 0:64, :] = s["D0"][0, p, :, :] * defect[0]
        return carry

    lax.fori_loop(7, 23, residual0, 0)
    pre0 = x

    down1(s["R0"], 7, 0, s["B1"])
    round1 = side1(s["B1"], 2)
    start(round1)

    wait(coarse)
    level1 = Level(1, 8, 48, 0.25)
    level2 = Level(1, 8, 48, 0.0625)
    level3 = Level(1, 8, 32, 0.015625, closed=True)
    level4 = Level(1, 8, 16, 0.00390625)
    down4(s["K3"], s["K4"])
    down4(s["S3"], s["S4"])

    def finish(level, name):
        def keep(t, p, diag, inverse):
            s["D" + name][t, p, level.window(), :] = diag
            s["I" + name][t, p, level.window(), :] = inverse

        return keep

    level1.coefficients(s["K1"], s["S1"], s["C1"], 2, 22, finish(level1, "1"))
    wait(round1)
    merge1(s["B1"], 2)
    round1 = main1(s["B1"], 6)
    start(round1)

    pack0(lambda i: pre0[0, 7 + i, 16:80, :], s["PN0"].at[0])
    side_n0 = sides(s["PN0"], s["ZN0"])
    start(side_n0)
    level2.coefficients(s["K2"], s["S2"], s["C2"], 1, 17, finish(level2, "2"))
    level3.coefficients(s["K3"], s["S3"], s["C3"], 1, 9, finish(level3, "3"))
    level4.coefficients(s["K4"], s["S4"], s["C4"], 1, 5, finish(level4, "4"))

    def begin(level, name, low, high):
        def body(p, carry):
            part = (0, p, level.window(), slice(None))
            scaled = s["B" + name][part] * s["I" + name][part]
            s["B" + name][part] = scaled
            s["XA" + name][part] = first_weight(name) * scaled
            return carry

        lax.fori_loop(low, high, body, 0)

    def first_weight(name):
        return cheb(BOTTOM_SWEEPS if name == "4" else SWEEPS)[0]

    wait(round1)
    begin(level1, "1", 2, 22)
    x, y = s["XA1"], s["XB1"]
    for t in range(1, SWEEPS):
        h = 6 - t
        level1.sweep(x, y, s["B1"], s["C1"], weights[t], 8 - h, 16 + h)
        x, y = y, x
    level1.residual(x, s["B1"], s["C1"], s["D1"], y, 8, 16)

    down2(y, s["B2"])
    round2 = side2(s["B2"], 2)
    start(round2)
    n32 = lane(32)
    for i in range(8):
        s["N1"][0, 8 + i, 16:48, :] = jnp.where(
            (n32 >= 32) & (n32 < 96), x[0, 8 + i, 16:48, :], 0.0
        )
    wait(round2)
    merge2(s["B2"], 2)
    round2 = main2(s["B2"])
    start(round2)
    side_n1 = side1(s["N1"], 3)
    start(side_n1)
    wait(round2)
    begin(level2, "2", 1, 17)
    x, y = s["XA2"], s["XB2"]
    for t in range(1, SWEEPS):
        level2.sweep(x, y, s["B2"], s["C2"], weights[t], 1, 17)
        x, y = y, x
    level2.residual(x, s["B2"], s["C2"], s["D2"], s["R2"], 1, 17)

    down3(s["R2"], 2)
    round3 = side3(2)
    start(round3)
    n16 = lane(16)
    for i in range(4):
        p = 1 + 4 * gx + i
        s["N2"][0, p, 24:40, :] = jnp.where((n16 >= 48) & (n16 < 80), x[0, p, 24:40, :], 0.0)
    wait(round3)
    merge3(s["B3"], 2)
    round3 = main3(s["B3"])
    start(round3)

    side_n2 = side2(s["N2"], 3)
    start(side_n2)
    wait(side_n0)
    for g in range(2):
        s["GN0"][0, 1 + g, 8:72, :] = jnp.where(
            (n64 % 16) < 8, s["ZN0"][0, 0, g], s["ZN0"][1, 0, g]
        )
    ghosts = ghost0(s["GN0"])
    wait(side_n1)
    merge1(s["N1"], 3)
    wait(side_n2)
    merge2(s["N2"], 3)
    wait(round3)
    main_n2 = main2(s["N2"])
    start(main_n2)
    main_n1 = main1(s["N1"], 6)
    start(main_n1)
    start(ghosts)
    for i in range(16):
        s["N0"][0, 7 + i, 16:80, :] = pre0[0, 7 + i, 16:80, :]
    main_n0 = main0(s["N0"], 7, s["N0"], 6)
    start(main_n0)

    begin(level3, "3", 1, 9)
    x, y = s["XA3"], s["XB3"]
    for t in range(1, SWEEPS):
        level3.sweep(x, y, s["B3"], s["C3"], weights[t], 1, 9)
        x, y = y, x
    level3.residual(x, s["B3"], s["C3"], s["D3"], s["R3"], 1, 9)
    down4(s["R3"], s["B4"])

    begin(level4, "4", 1, 5)
    u, v = s["XA4"], s["XB4"]
    for weight in cheb(BOTTOM_SWEEPS)[1:]:
        level4.sweep(u, v, s["B4"], s["C4"], weight, 1, 5)
        u, v = v, u

    def spread(rows, planes, matrix, load, dst):
        value = product(jnp.concatenate([load(i) for i in range(planes)], axis=0), matrix)
        for i in range(planes):
            part = value[i * rows : (i + 1) * rows, :]
            dst[i, pl.ds(0, rows, stride=2), :] = part
            dst[i, pl.ds(1, rows, stride=2), :] = part

    fine = s["T"]
    spread(16, 4, doubling(0, 0, 0, 128), lambda i: u[0, 1 + i, 8:24, :], fine)
    for i in range(8):
        y[0, 1 + i, 8:40, :] = x[0, 1 + i, 8:40, :] + fine[i // 2, 0:32, :]
    for t in range(SWEEPS):
        x, y = y, x
        level3.sweep(x, y, s["B3"], s["C3"], weights[t], 1, 9)
    e3 = y

    wait(main_n2)
    rows3 = pl.ds(pl.multiple_of(8 * gy, 8), 24)
    spread(24, 8, doubling(16 * gz, 48, 16, 112), lambda i: e3[0, 1 + i, rows3, :], fine)
    y, x = s["XA2"], s["XB2"]
    for i in range(16):
        y[0, 1 + i, 8:56, :] = s["N2"][0, 1 + i, 8:56, :] + fine[i // 2, 0:48, :]
    for t in range(SWEEPS):
        x, y = y, x
        level2.sweep(x, y, s["B2"], s["C2"], weights[t], 1, 17)
    e2 = y

    wait(main_n1)
    value = product(
        jnp.concatenate([e2[0, 1 + i, 20:44, :] for i in range(16)], axis=0),
        doubling(48, 32, 24, 104),
    )
    fine1 = s["T1"]
    pl.when(gx == 0)(lambda: clear(fine1, pl.ds(0, 4)))
    pl.when(gx == nx - 1)(lambda: clear(fine1, pl.ds(20, 4)))
    for i in range(16):
        part = value[i * 24 : (i + 1) * 24, :]
        fine1[4 + i, pl.ds(0, 24, stride=2), :] = part
        fine1[4 + i, pl.ds(1, 24, stride=2), :] = part
    y, x = s["XA1"], s["XB1"]
    for p in range(-6, 14):
        y[0, 8 + p, 8:56, :] = s["N1"][0, 8 + p, 8:56, :] + fine1[4 + 4 * gx + p // 2, 0:48, :]
    for t in range(SWEEPS):
        x, y = y, x
        h = 5 - t
        level1.sweep(x, y, s["B1"], s["C1"], weights[t], 8 - h, 16 + h)
    for i in range(8):
        s["E1"][0, 8 + i, 16:48, :] = jnp.where(
            (n32 >= 32) & (n32 < 96), y[0, 8 + i, 16:48, :], 0.0
        )
    round1 = side1(s["E1"], 4)
    start(round1)
    wait(ghosts)
    unpack0(s["GN0"].at[0], s["N0"])
    wait(round1)
    merge1(s["E1"], 4)
    round1 = main1(s["E1"], 3)
    start(round1)
    wait(main_n0)
    wait(round1)

    to_main = doubling(32, 0, 0, 128)
    to_side = doubling(32, -128, 0, 8) + doubling(32, 128, 120, 128)
    xa0 = s["S0"]
    for i in range(14):
        e = s["E1"][0, 5 + i, 12:52, :]
        for t, matrix in ((0, to_main), (1, to_side)):
            part = product(e, matrix)
            s["T0"][t, pl.ds(0, 40, stride=2), :] = part
            s["T0"][t, pl.ds(1, 40, stride=2), :] = part
            for o in range(2):
                p = 1 + 2 * i + o
                xa0[t, p, 8:88, :] = s["N0"][t, p, 8:88, :] + s["T0"][t, 0:80, :]
    x, y = s["XB0"], xa0
    for t in range(SWEEPS - 1):
        x, y = y, x
        h = 5 - t
        level0.sweep(x, y, b0, c0, weights[t], 7 - h, 23 + h)

    def last(p, carry):
        mid, defect = inside0.defect(y, b0, c0, p, 1)
        out[p - 7, :, :] = mid[0] + weights[SWEEPS - 1] * defect[0]
        return carry

    lax.fori_loop(7, 23, last, 0)


def scratch():
    shapes = {}
    for name in ("K0", "S0", "B0", "N0", "XB0"):
        shapes[name] = (2, 30, 96, 128)
    shapes["C0"] = (6, 2, 30, 96, 128)
    shapes["D0"], shapes["R0"] = (1, 30, 64, 128), (1, 23, 72, 128)
    shapes["P0"], shapes["Z0"], shapes["G0"] = (3, 2, 64, 128), (2, 3, 2, 64, 128), (3, 4, 80, 128)
    shapes["PN0"], shapes["ZN0"] = (1, 2, 64, 128), (2, 1, 2, 64, 128)
    shapes["GN0"] = (1, 4, 80, 128)
    shapes["T0"] = (2, 88, 128)
    for level, dims in (("1", (24, 64, 128)), ("2", (18, 64, 128)), ("3", (10, 48, 128)), ("4", (6, 32, 128))):
        for name in ("K", "S", "B", "I", "D", "XA", "XB"):
            shapes[name + level] = (1,) + dims
        shapes["C" + level] = (6, 1) + dims
    shapes["N1"] = shapes["E1"] = shapes["K1"]
    shapes["N2"] = shapes["R2"] = shapes["K2"]
    shapes["R3"] = shapes["K3"]
    shapes["P1"], shapes["Z1"] = (5, 32, 128), (5, 2, 32, 128)
    shapes["Z2"] = (4, 2, 4, 16, 128)
    shapes["Z3"] = (3, 8, 2, 8, 128)
    shapes["T"], shapes["T1"] = (8, 56, 128), (24, 56, 128)
    return {
        "send": pltpu.SemaphoreType.DMA((COPIES,)),
        "recv": pltpu.SemaphoreType.DMA((COPIES,)),
        "local": pltpu.SemaphoreType.DMA((3,)),
        **{name: pltpu.VMEM(shape, F32) for name, shape in shapes.items()},
    }


def on_device(rhs, kappa, sigma):
    return pl.pallas_call(
        kernel,
        out_shape=jax.ShapeDtypeStruct(rhs.shape, F32),
        in_specs=[pl.BlockSpec(memory_space=pl.ANY)] * 3,
        out_specs=pl.BlockSpec(memory_space=pltpu.VMEM),
        scratch_shapes=[scratch()],
        compiler_params=pltpu.CompilerParams(
            collective_id=0, has_side_effects=True, vmem_limit_bytes=63 * 2**20
        ),
    )(rhs, kappa, sigma)


def solution(mesh):
    placed = (P("gx", "gy", "gz"), P("gx", "gy", "gz"), P("gx", "gy", "gz"))
    return jax.shard_map(
        on_device, mesh=mesh, in_specs=placed, out_specs=P("gx", "gy", "gz"), check_vma=False
    )
```

time: 1690 us -> 162 us (0.10); the launches traced: 1670 us -> 162 us
  starting transfers between devices: 910 us -> 0 us
  waiting for transfers between devices: 365 us -> 0 us
  local copies, waits for them, and re-layouts: 244 us -> 1.89 us
  Pallas kernels: 0 us -> 160 us
  other arithmetic: 144 us -> 0 us
    ppermute x360 -> x0, starting transfers between devices: 910 us -> none  [the longest x180 627 us: with_halo(): lax.ppermute(lax.slice_in_dim(block, block.shape[dim] - width, None, axis...]
    ppermute x360 -> x0, waiting for transfers between devices: 365 us -> none  [the longest x180 327 us: with_halo(): lax.ppermute(lax.slice_in_dim(block, 0, width, axis=dim), axis, backward)]
    pallas_call x0 -> x1, Pallas kernels: none -> 160 us  [on_device(): pl.pallas_call(kernel, out_shape=jax.ShapeDtypeStruct(rhs.shape, F32), in...]
    reshape x11 -> x0, local copies, waits for them, and re-layouts: 118 us -> none  [the longest x5 112 us: restrict(): field.reshape(n0 // 2, 2, n1 // 2, 2, n2 // 2, 2).mean(axis=(1, 3, 5))]
    add x55 -> x0, other arithmetic: 60.6 us -> none  [the longest x51 58.2 us: relax(): guess = guess + weight * (rhs - image) / diag]
    reduce_sum x15 -> x0, other arithmetic: 56 us -> none  [restrict(): field.reshape(n0 // 2, 2, n1 // 2, 2, n2 // 2, 2).mean(axis=(1, 3, 5))]
    unnamed x118 -> x1, local copies, waits for them, and re-layouts: 38.7 us -> 1.89 us
    ppermute x26 -> x0, local copies, waits for them, and re-layouts: 30.8 us -> none  [the longest x13 17.3 us: with_halo(): lax.ppermute(lax.slice_in_dim(block, block.shape[dim] - width, None, axis...]
  transfers between devices with their start and end apart: 360 -> 0, of which waited for: 161 -> 0; matrix products, arithmetic and copies ran while one was open for 15% -> 0% of each run, Pallas kernels for 0% -> 0%
where the time goes in v1:
time: 162 us
  Pallas kernels  160 us (99%)
  local copies, waits for them, and re-layouts  1.89 us (1%)
    pallas_call x1, Pallas kernels, on_device(): pl.pallas_call(kernel, out_shape=jax.ShapeDtypeStruct(rhs.shape, F32), in...  160 us

profile of v1, /device:TPU:1, one launch (start us, length us, event | category | flops | bytes accessed | tf_op | source)
XLA Modules:
  0.0 162.3 jit_solution(9429887584640662125)
XLA Ops:
  0.0 160.4 %shard_map.37 = f32[16,64,128]{2,1,0:T(8,128)} custom-call(f32[16,64,128]{2,1,0:T(8,128)} %rhs.1, f32[16,64,128]{2,1,0:T(8,128)} %kappa.1, f32[16,64,128]{2,1,0:T(8,128)} %sigma.1), custom_call_target="tpu_custom_call" | custom-call | tf_op jit(solution)/shard_map/pallas_call | solution.py:758
  160.4 1.9 %copy.5 = f32[16,64,128]{2,1,0:T(8,128)} copy(f32[16,64,128]{2,1,0:T(8,128)} %shard_map.37) | data formatting | bytes 1048576

commit v2 on v1

--- a/solution.py
+++ b/solution.py
@@ -94,15 +94,28 @@
     return a if b is None else a & b
 
 
+def groups(low, high, size, action):
+    whole = (high - low) // size
+    if whole == 1:
+        action(low, size)
+    elif whole:
+
+        def body(i, carry):
+            action(low + size * i, size)
+            return carry
+
+        lax.fori_loop(0, whole, body, 0)
+    rest = (high - low) % size
+    if rest:
+        action(high - rest, rest)
+
+
 class Level:
-    def __init__(self, tiles, row0, rows, scale, closed=False):
-        self.tiles, self.row0, self.rows, self.scale, self.closed = tiles, row0, rows, scale, closed
-
-    def window(self, shift=0):
-        return pl.ds(self.row0 + shift, self.rows)
+    def __init__(self, tiles, scale, closed=False):
+        self.tiles, self.scale, self.closed = tiles, scale, closed
 
     def beside(self, values):
-        n = lane(self.rows)
+        n = lane(values[0].shape[0])
         left = [turn(v, 1) for v in values]
         right = [turn(v, -1) for v in values]
         if self.tiles == 2:
@@ -110,71 +123,73 @@
             right = [jnp.where(n == 127, right[1 - t], right[t]) for t in range(2)]
         return left, right
 
-    def near(self, ref, p, tiles):
-        mid = [ref[t, p, self.window(), :] for t in range(self.tiles)]
-        left, right = self.beside(mid)
-        return mid, [
-            (
-                ref[t, p + 1, self.window(), :],
-                ref[t, p - 1, self.window(), :],
-                ref[t, p, self.window(1), :],
-                ref[t, p, self.window(-1), :],
-                left[t],
-                right[t],
-            )
-            for t in range(tiles)
-        ]
-
-    def coefficients(self, kappa, sigma, coef, low, high, finish):
-        n = lane(self.rows)
-
-        def body(p, carry):
-            mid, around = self.near(kappa, p, self.tiles)
-            for t in range(self.tiles):
-                k, near = mid[t], list(around[t])
-                if self.closed:
-                    near[4] = jnp.where(n == 0, 0.0, near[4])
-                    near[5] = jnp.where(n == 127, 0.0, near[5])
-                face = [(0.5 * self.scale) * (k + j) for j in near]
-                diag = face[0] + face[1] + face[2] + face[3] + face[4] + face[5]
-                diag = diag + sigma[t, p, self.window(), :]
-                inverse = jnp.where(k > 0.0, 1.0 / diag, 0.0)
-                if self.closed:
-                    face[4] = jnp.where(n == 0, 0.0, face[4])
-                    face[5] = jnp.where(n == 127, 0.0, face[5])
-                for j in range(6):
-                    coef[j, t, p, self.window(), :] = face[j] * inverse
-                finish(t, p, diag, inverse)
-            return carry
-
-        lax.fori_loop(low, high, body, 0)
-
-    def defect(self, x, rhs, coef, p, tiles):
-        mid, around = self.near(x, p, tiles)
-        out = []
-        for t in range(tiles):
-            total = rhs[t, p, self.window(), :] - mid[t]
-            for j in range(6):
-                total = total + coef[j, t, p, self.window(), :] * around[t][j]
-            out.append(total)
-        return mid, out
-
-    def sweep(self, src, dst, rhs, coef, weight, low, high):
-        def body(p, carry):
-            mid, out = self.defect(src, rhs, coef, p, self.tiles)
-            for t in range(self.tiles):
-                dst[t, p, self.window(), :] = mid[t] + weight * out[t]
-            return carry
-
-        lax.fori_loop(low, high, body, 0)
-
-    def residual(self, x, rhs, coef, diag, dst, low, high):
-        def body(p, carry):
-            _, out = self.defect(x, rhs, coef, p, 1)
-            dst[0, p, self.window(), :] = diag[0, p, self.window(), :] * out[0]
-            return carry
-
-        lax.fori_loop(low, high, body, 0)
+    def around(self, ref, p, count, row, rows, tiles):
+        win = pl.ds(row, rows)
+        mid = [[ref[t, p + i - 1, win, :] for i in range(count + 2)] for t in range(tiles)]
+        mid += [[None] + [ref[t, p + i, win, :] for i in range(count)] for t in range(tiles, self.tiles)]
+        found = []
+        for i in range(count):
+            left, right = self.beside([mid[t][i + 1] for t in range(self.tiles)])
+            for t in range(tiles):
+                near = [
+                    mid[t][i + 2],
+                    mid[t][i],
+                    ref[t, p + i, pl.ds(row + 1, rows), :],
+                    ref[t, p + i, pl.ds(row - 1, rows), :],
+                    left[t],
+                    right[t],
+                ]
+                found.append((t, p + i, mid[t][i + 1], near))
+        return found
+
+    def coefficients(self, kappa, sigma, coef, low, high, size, row, rows, chunk, finish):
+        def block(first, count):
+            for start_row in range(row, row + rows, chunk):
+                win = pl.ds(start_row, chunk)
+                n = lane(chunk)
+                for t, p, k, near in self.around(kappa, first, count, start_row, chunk, self.tiles):
+                    if self.closed:
+                        near[4] = jnp.where(n == 0, 0.0, near[4])
+                        near[5] = jnp.where(n == 127, 0.0, near[5])
+                    face = [(0.5 * self.scale) * (k + j) for j in near]
+                    diag = (face[0] + face[1]) + (face[2] + face[3]) + (face[4] + face[5])
+                    diag = diag + sigma[t, p, win, :]
+                    inverse = jnp.where(k > 0.0, 1.0 / diag, 0.0)
+                    if self.closed:
+                        face[4] = jnp.where(n == 0, 0.0, face[4])
+                        face[5] = jnp.where(n == 127, 0.0, face[5])
+                    for j in range(6):
+                        coef[j, t, p, win, :] = face[j] * inverse
+                    finish(t, p, start_row, chunk, diag, inverse)
+
+        groups(low, high, size, block)
+
+    def defects(self, x, rhs, coef, low, high, size, row, rows, chunk, tiles, use):
+        def block(first, count):
+            for start_row in range(row, row + rows, chunk):
+                win = pl.ds(start_row, chunk)
+                found = []
+                for t, p, mid, near in self.around(x, first, count, start_row, chunk, tiles):
+                    c = [coef[j, t, p, win, :] for j in range(6)]
+                    a = (c[0] * near[0] + c[1] * near[1]) + (c[2] * near[2] + c[3] * near[3])
+                    b = (rhs[t, p, win, :] - mid) + (c[4] * near[4] + c[5] * near[5])
+                    found.append((t, p, mid, a + b))
+                for t, p, mid, value in found:
+                    use(t, p, start_row, chunk, mid, value)
+
+        groups(low, high, size, block)
+
+    def sweep(self, src, dst, rhs, coef, weight, low, high, size, row, rows, chunk):
+        def use(t, p, r, n, mid, value):
+            dst[t, p, pl.ds(r, n), :] = mid + weight * value
+
+        self.defects(src, rhs, coef, low, high, size, row, rows, chunk, self.tiles, use)
+
+    def residual(self, x, rhs, coef, diag, dst, low, high, size, row, rows, chunk):
+        def use(t, p, r, n, mid, value):
+            dst[0, p, pl.ds(r, n), :] = diag[0, p, pl.ds(r, n), :] * value
+
+        self.defects(x, rhs, coef, low, high, size, row, rows, chunk, 1, use)
 
 
 def restrict(load, planes, matrix, store):
@@ -487,52 +502,57 @@
     wait(mains)
 
     weights = cheb(SWEEPS)
-    level0 = Level(2, 8, 80, 1.0)
+    level0 = Level(2, 1.0)
     c0, b0, xa0, xb0 = s["C0"], s["B0"], s["S0"], s["XB0"]
 
-    def finish0(t, p, diag, inverse):
-        scaled = b0[t, p, 8:88, :] * inverse
-        b0[t, p, 8:88, :] = scaled
-        xa0[t, p, 8:88, :] = weights[0] * scaled
+    def finish0(t, p, r, n, diag, inverse):
+        win = pl.ds(r, n)
+        scaled = b0[t, p, win, :] * inverse
+        b0[t, p, win, :] = scaled
+        xa0[t, p, win, :] = weights[0] * scaled
         if t == 0:
-            s["D0"][0, p, :, :] = diag[8:72, :]
-
-    level0.coefficients(s["K0"], s["S0"], c0, 1, 29, finish0)
+            s["D0"][0, p, win, :] = diag
+
+    def rows0(h):
+        return (8, 80, 16) if h > 4 else (12, 72, 24) if h > 0 else (16, 64, 16)
+
+    level0.coefficients(s["K0"], s["S0"], c0, 1, 29, 4, 8, 80, 16, finish0)
     x, y = xa0, xb0
     for t in range(1, SWEEPS):
-        level0.sweep(x, y, b0, c0, weights[t], 7 - (6 - t), 23 + (6 - t))
+        h = 6 - t
+        level0.sweep(x, y, b0, c0, weights[t], 7 - h, 23 + h, 8 + h, *rows0(h))
         x, y = y, x
-
-    inside0 = Level(2, 16, 64, 1.0)
-
-    def residual0(p, carry):
-        _, defect = inside0.defect(x, b0, c0, p, 1)
-        s["R0"][0, p, 0:64, :] = s["D0"][0, p, :, :] * defect[0]
-        return carry
-
-    lax.fori_loop(7, 23, residual0, 0)
+    level0.residual(x, b0, c0, s["D0"], s["R0"], 7, 23, 8, *rows0(0))
     pre0 = x
 
-    down1(s["R0"], 7, 0, s["B1"])
+    down1(s["R0"], 7, 16, s["B1"])
     round1 = side1(s["B1"], 2)
     start(round1)
 
     wait(coarse)
-    level1 = Level(1, 8, 48, 0.25)
-    level2 = Level(1, 8, 48, 0.0625)
-    level3 = Level(1, 8, 32, 0.015625, closed=True)
-    level4 = Level(1, 8, 16, 0.00390625)
+    level1 = Level(1, 0.25)
+    level2 = Level(1, 0.0625)
+    level3 = Level(1, 0.015625, closed=True)
+    level4 = Level(1, 0.00390625)
+    all3, all4 = (1, 9, 8, 8, 32, 32), (1, 5, 4, 8, 16, 16)
+
+    def part1(h):
+        return (8 - h, 16 + h, 8 + 2 * h) + ((8, 48, 48) if h > 4 else (12, 40, 40))
+
+    def part2(h):
+        return (1, 17, 16) + ((16, 32, 32) if h > 4 else (20, 24, 24))
+
     down4(s["K3"], s["K4"])
     down4(s["S3"], s["S4"])
 
-    def finish(level, name):
-        def keep(t, p, diag, inverse):
-            s["D" + name][t, p, level.window(), :] = diag
-            s["I" + name][t, p, level.window(), :] = inverse
+    def finish(name):
+        def keep(t, p, r, n, diag, inverse):
+            s["D" + name][t, p, pl.ds(r, n), :] = diag
+            s["I" + name][t, p, pl.ds(r, n), :] = inverse
 
         return keep
 
-    level1.coefficients(s["K1"], s["S1"], s["C1"], 2, 22, finish(level1, "1"))
+    level1.coefficients(s["K1"], s["S1"], s["C1"], 2, 22, 5, 8, 48, 48, finish("1"))
     wait(round1)
     merge1(s["B1"], 2)
     round1 = main1(s["B1"], 6)
@@ -541,31 +561,31 @@
     pack0(lambda i: pre0[0, 7 + i, 16:80, :], s["PN0"].at[0])
     side_n0 = sides(s["PN0"], s["ZN0"])
     start(side_n0)
-    level2.coefficients(s["K2"], s["S2"], s["C2"], 1, 17, finish(level2, "2"))
-    level3.coefficients(s["K3"], s["S3"], s["C3"], 1, 9, finish(level3, "3"))
-    level4.coefficients(s["K4"], s["S4"], s["C4"], 1, 5, finish(level4, "4"))
-
-    def begin(level, name, low, high):
-        def body(p, carry):
-            part = (0, p, level.window(), slice(None))
-            scaled = s["B" + name][part] * s["I" + name][part]
-            s["B" + name][part] = scaled
-            s["XA" + name][part] = first_weight(name) * scaled
-            return carry
-
-        lax.fori_loop(low, high, body, 0)
+    level2.coefficients(s["K2"], s["S2"], s["C2"], 1, 17, 8, 16, 32, 32, finish("2"))
+    level3.coefficients(s["K3"], s["S3"], s["C3"], *all3, finish("3"))
+    level4.coefficients(s["K4"], s["S4"], s["C4"], *all4, finish("4"))
+
+    def begin(name, low, high, size, row, rows, chunk):
+        def block(first, count):
+            for i in range(count):
+                part = (0, first + i, pl.ds(row, rows), slice(None))
+                scaled = s["B" + name][part] * s["I" + name][part]
+                s["B" + name][part] = scaled
+                s["XA" + name][part] = first_weight(name) * scaled
+
+        groups(low, high, size, block)
 
     def first_weight(name):
         return cheb(BOTTOM_SWEEPS if name == "4" else SWEEPS)[0]
 
     wait(round1)
-    begin(level1, "1", 2, 22)
+    begin("1", *part1(6))
     x, y = s["XA1"], s["XB1"]
     for t in range(1, SWEEPS):
         h = 6 - t
-        level1.sweep(x, y, s["B1"], s["C1"], weights[t], 8 - h, 16 + h)
+        level1.sweep(x, y, s["B1"], s["C1"], weights[t], *part1(h))
         x, y = y, x
-    level1.residual(x, s["B1"], s["C1"], s["D1"], y, 8, 16)
+    level1.residual(x, s["B1"], s["C1"], s["D1"], y, 8, 16, 8, 16, 32, 32)
 
     down2(y, s["B2"])
     round2 = side2(s["B2"], 2)
@@ -582,12 +602,12 @@
     side_n1 = side1(s["N1"], 3)
     start(side_n1)
     wait(round2)
-    begin(level2, "2", 1, 17)
+    begin("2", *part2(6))
     x, y = s["XA2"], s["XB2"]
     for t in range(1, SWEEPS):
-        level2.sweep(x, y, s["B2"], s["C2"], weights[t], 1, 17)
+        level2.sweep(x, y, s["B2"], s["C2"], weights[t], *part2(6 - t))
         x, y = y, x
-    level2.residual(x, s["B2"], s["C2"], s["D2"], s["R2"], 1, 17)
+    level2.residual(x, s["B2"], s["C2"], s["D2"], s["R2"], 1, 17, 16, 24, 16, 16)
 
     down3(s["R2"], 2)
     round3 = side3(2)
@@ -624,18 +644,18 @@
     main_n0 = main0(s["N0"], 7, s["N0"], 6)
     start(main_n0)
 
-    begin(level3, "3", 1, 9)
+    begin("3", *all3)
     x, y = s["XA3"], s["XB3"]
     for t in range(1, SWEEPS):
-        level3.sweep(x, y, s["B3"], s["C3"], weights[t], 1, 9)
+        level3.sweep(x, y, s["B3"], s["C3"], weights[t], *all3)
         x, y = y, x
-    level3.residual(x, s["B3"], s["C3"], s["D3"], s["R3"], 1, 9)
+    level3.residual(x, s["B3"], s["C3"], s["D3"], s["R3"], *all3)
     down4(s["R3"], s["B4"])
 
-    begin(level4, "4", 1, 5)
+    begin("4", *all4)
     u, v = s["XA4"], s["XB4"]
     for weight in cheb(BOTTOM_SWEEPS)[1:]:
-        level4.sweep(u, v, s["B4"], s["C4"], weight, 1, 5)
+        level4.sweep(u, v, s["B4"], s["C4"], weight, *all4)
         u, v = v, u
 
     def spread(rows, planes, matrix, load, dst):
@@ -651,7 +671,7 @@
         y[0, 1 + i, 8:40, :] = x[0, 1 + i, 8:40, :] + fine[i // 2, 0:32, :]
     for t in range(SWEEPS):
         x, y = y, x
-        level3.sweep(x, y, s["B3"], s["C3"], weights[t], 1, 9)
+        level3.sweep(x, y, s["B3"], s["C3"], weights[t], *all3)
     e3 = y
 
     wait(main_n2)
@@ -659,10 +679,10 @@
     spread(24, 8, doubling(16 * gz, 48, 16, 112), lambda i: e3[0, 1 + i, rows3, :], fine)
     y, x = s["XA2"], s["XB2"]
     for i in range(16):
-        y[0, 1 + i, 8:56, :] = s["N2"][0, 1 + i, 8:56, :] + fine[i // 2, 0:48, :]
+        y[0, 1 + i, 12:52, :] = s["N2"][0, 1 + i, 12:52, :] + fine[i // 2, 4:44, :]
     for t in range(SWEEPS):
         x, y = y, x
-        level2.sweep(x, y, s["B2"], s["C2"], weights[t], 1, 17)
+        level2.sweep(x, y, s["B2"], s["C2"], weights[t], *part2(8 - t))
     e2 = y
 
     wait(main_n1)
@@ -683,7 +703,7 @@
     for t in range(SWEEPS):
         x, y = y, x
         h = 5 - t
-        level1.sweep(x, y, s["B1"], s["C1"], weights[t], 8 - h, 16 + h)
+        level1.sweep(x, y, s["B1"], s["C1"], weights[t], *part1(h))
     for i in range(8):
         s["E1"][0, 8 + i, 16:48, :] = jnp.where(
             (n32 >= 32) & (n32 < 96), y[0, 8 + i, 16:48, :], 0.0
@@ -715,14 +735,12 @@
     for t in range(SWEEPS - 1):
         x, y = y, x
         h = 5 - t
-        level0.sweep(x, y, b0, c0, weights[t], 7 - h, 23 + h)
-
-    def last(p, carry):
-        mid, defect = inside0.defect(y, b0, c0, p, 1)
-        out[p - 7, :, :] = mid[0] + weights[SWEEPS - 1] * defect[0]
-        return carry
-
-    lax.fori_loop(7, 23, last, 0)
+        level0.sweep(x, y, b0, c0, weights[t], 7 - h, 23 + h, 8 + h, *rows0(h))
+
+    def last(t, p, r, n, mid, value):
+        out[p - 7, pl.ds(r - 16, n), :] = mid + weights[SWEEPS - 1] * value
+
+    level0.defects(y, b0, c0, 7, 23, 8, *rows0(0), 1, last)
 
 
 def scratch():
@@ -730,7 +748,7 @@
     for name in ("K0", "S0", "B0", "N0", "XB0"):
         shapes[name] = (2, 30, 96, 128)
     shapes["C0"] = (6, 2, 30, 96, 128)
-    shapes["D0"], shapes["R0"] = (1, 30, 64, 128), (1, 23, 72, 128)
+    shapes["D0"], shapes["R0"] = (1, 30, 96, 128), (1, 23, 88, 128)
     shapes["P0"], shapes["Z0"], shapes["G0"] = (3, 2, 64, 128), (2, 3, 2, 64, 128), (3, 4, 80, 128)
     shapes["PN0"], shapes["ZN0"] = (1, 2, 64, 128), (2, 1, 2, 64, 128)
     shapes["GN0"] = (1, 4, 80, 128)

time: 162 us -> 117 us (0.72)
  Pallas kernels: 160 us -> 115 us
    pallas_call x1, Pallas kernels: 160 us -> 115 us  [on_device(): pl.pallas_call(kernel, out_shape=jax.ShapeDtypeStruct(rhs.shape, F32), in...]
where the time goes in v2:
time: 117 us; the launch traced here: 116 us
  Pallas kernels  115 us (98%)
  local copies, waits for them, and re-layouts  1.89 us (2%)
    pallas_call x1, Pallas kernels, on_device(): pl.pallas_call(kernel, out_shape=jax.ShapeDtypeStruct(rhs.shape, F32), in...  115 us

profile of v2, /device:TPU:1, one launch (start us, length us, event | category | flops | bytes accessed | tf_op | source)
XLA Modules:
  0.0 116.5 jit_solution(6861555843818058457)
XLA Ops:
  0.0 114.6 %shard_map.37 = f32[16,64,128]{2,1,0:T(8,128)} custom-call(f32[16,64,128]{2,1,0:T(8,128)} %rhs.1, f32[16,64,128]{2,1,0:T(8,128)} %kappa.1, f32[16,64,128]{2,1,0:T(8,128)} %sigma.1), custom_call_target="tpu_custom_call" | custom-call | tf_op jit(solution)/shard_map/pallas_call | solution.py:776
  114.6 1.9 %copy.5 = f32[16,64,128]{2,1,0:T(8,128)} copy(f32[16,64,128]{2,1,0:T(8,128)} %shard_map.37) | data formatting | bytes 1048576

commit v3 on v2

--- a/solution.py
+++ b/solution.py
@@ -13,7 +13,7 @@
 BOTTOM_SWEEPS = 8
 MESH = pl.DeviceIdType.MESH
 F32 = jnp.float32
-COPIES = 256
+COPIES = 148
 
 
 def cheb(count):
@@ -55,9 +55,10 @@
     def __init__(self, send, recv):
         self.send, self.recv, self.used = send, recv, 0
 
-    def copy(self, src, dst, target, send_ok=None, recv_ok=None):
-        k = self.used
-        self.used += 1
+    def copy(self, src, dst, target, send_ok=None, recv_ok=None, k=None):
+        if k is None:
+            k = self.used
+            self.used += 1
         made = pltpu.make_async_remote_copy(
             src_ref=src,
             dst_ref=dst,
@@ -207,6 +208,10 @@
     gx, gy, gz = lax.axis_index("gx"), lax.axis_index("gy"), lax.axis_index("gz")
     nx, ny, nz = 4, 4, 8
     links = Links(s["send"], s["recv"])
+    s = dict(s)
+    for level in "123":
+        s["K" + level] = s["KS" + level].at[pl.ds(0, 1)]
+        s["S" + level] = s["KS" + level].at[pl.ds(1, 1)]
     has = {
         ("x", 1): gx < nx - 1,
         ("x", -1): gx > 0,
@@ -233,9 +238,9 @@
         clear_edges(s[name], (7, 23), (8, 8, 80))
     for name in ("K1", "S1", "B1", "N1", "E1"):
         clear_edges(s[name], (8, 16), (8, 8, 48))
-    for name in ("K2", "S2", "B2", "N2"):
-        pl.when(gy == 0)(lambda ref=s[name]: clear(ref, 0, slice(None), pl.ds(8, 16)))
-        pl.when(gy == ny - 1)(lambda ref=s[name]: clear(ref, 0, slice(None), pl.ds(40, 16)))
+    every = slice(None)
+    pl.when(gy == 0)(lambda: clear(s["Q2"], every, every, every, pl.ds(0, 16)))
+    pl.when(gy == ny - 1)(lambda: clear(s["Q2"], every, every, every, pl.ds(32, 16)))
     for name in ("K2", "XA2", "XB2"):
         clear(s[name], 0, 0)
         clear(s[name], 0, 17)
@@ -264,13 +269,12 @@
     line_mates = [(gx, gy, lax.rem(gz + i, nz)) for i in range(1, nz)]
     for mate in plane_mates + line_mates:
         pl.semaphore_signal(barrier, inc=1, device_id=mate, device_id_type=MESH)
-    pl.semaphore_wait(barrier, len(plane_mates + line_mates))
 
     around = [(dx, dy) for dx in (1, -1, 0) for dy in (0, 1, -1) if dx or dy]
 
-    def neighbours(make):
+    def neighbours(make, first=None):
         copies = []
-        for dx, dy in around:
+        for m, (dx, dy) in enumerate(around):
             src, dst = make(dx, dy)
             copies.append(
                 links.copy(
@@ -279,6 +283,7 @@
                     (gx + dx, gy + dy, gz),
                     both(has["x", dx], has["y", dy]),
                     both(has["x", -dx], has["y", -dy]),
+                    None if first is None else first + m,
                 )
             )
         return copies
@@ -289,7 +294,7 @@
             links.copy(src, slots.at[1], (gx, gy, gz - 1), has["z", -1], has["z", 1]),
         ]
 
-    def main0(src, first, ref, h):
+    def main0(src, first, ref, h, k=None):
         def make(dx, dy):
             sp = {1: (first + 16 - h, h), -1: (first, h), 0: (first, 16)}[dx]
             dp = {1: (7 - h, h), -1: (23, h), 0: (7, 16)}[dx]
@@ -301,7 +306,7 @@
             ]
             return source, ref.at[0, pl.ds(*dp), pl.ds(*dr)]
 
-        return neighbours(make)
+        return neighbours(make, k)
 
     inner = [
         pltpu.make_async_copy(src, s[name].at[0, pl.ds(7, 16), pl.ds(16, 64)], s["local"].at[k])
@@ -309,8 +314,8 @@
     ]
     for made in inner:
         made.start()
-    mains = main0(kappa, 0, s["K0"], 7) + main0(sigma, 0, s["S0"], 6) + main0(rhs, 0, s["B0"], 6)
-    start(mains)
+    mains = main0(kappa, 0, s["K0"], 7) + main0(sigma, 0, s["S0"], 6)
+    main_b = main0(rhs, 0, s["B0"], 6)
     for made in inner:
         made.wait()
 
@@ -326,6 +331,9 @@
     for a, name in enumerate(("K0", "S0", "B0")):
         pack0(lambda i, ref=s[name]: ref[0, 7 + i, 16:80, :], s["P0"].at[a])
     side0 = sides(s["P0"], s["Z0"])
+    pl.semaphore_wait(barrier, len(plane_mates + line_mates))
+    start(mains)
+    start(main_b)
     start(side0)
 
     to1 = halving(0, 32, 64)
@@ -350,7 +358,7 @@
 
     def down3(src, use):
         def store(i, v):
-            s["Z3"][use, gz, i, :, :] = v
+            s["Z3"][gz, use, i, :, :] = v
 
         restrict(
             lambda i, o: src[0, 1 + 4 * gx + i, pl.ds(24 + o, 8, stride=2), :], 2, to3, store
@@ -362,7 +370,7 @@
 
         restrict(lambda i, o: src[0, 1 + i, pl.ds(8 + o, 16, stride=2), :], 4, to4, store)
 
-    def side1(ref, use):
+    def pack1(ref, use):
         n = lane(32)
         total = jnp.zeros((32, 128), F32)
         for q in range(8):
@@ -370,11 +378,14 @@
             v = turn(v + turn(v, 64), 16 * q - 24)
             total = jnp.where((n >= 16 * q) & (n < 16 * q + 16), v, total)
         s["P1"][use, :, :] = total
-        return sides(s["P1"].at[use], s["Z1"].at[use])
+
+    def side1(use, count=1):
+        part = pl.ds(use, count)
+        return sides(s["P1"].at[part], s["Z1"].at[:, part])
 
     def merge1(ref, use):
         n = lane(32)
-        ghosts = jnp.where((n % 16) < 8, s["Z1"][use, 0], s["Z1"][use, 1])
+        ghosts = jnp.where((n % 16) < 8, s["Z1"][0, use], s["Z1"][1, use])
         for q in range(8):
             low = turn(ghosts, 24 - 16 * q)
             high = turn(ghosts, 24 - 16 * q + 64)
@@ -382,75 +393,90 @@
             v = jnp.where((n >= 24) & (n < 32), low, v)
             ref[0, 8 + q, 16:48, :] = jnp.where((n >= 96) & (n < 104), high, v)
 
-    def main1(ref, h):
+    def main1(ref, h, k=None):
         def make(dx, dy):
             sp = {1: (16 - h, h), -1: (8, h), 0: (8, 8)}[dx]
             dp = {1: (8 - h, h), -1: (16, h), 0: (8, 8)}[dx]
             sr = {1: (40, 8), -1: (16, 8), 0: (16, 32)}[dy]
             dr = {1: (8, 8), -1: (48, 8), 0: (16, 32)}[dy]
-            return ref.at[0, pl.ds(*sp), pl.ds(*sr)], ref.at[0, pl.ds(*dp), pl.ds(*dr)]
-
-        return neighbours(make)
-
-    def side2(ref, use):
-        return sides(ref.at[0, own2, pl.ds(24, 16)], s["Z2"].at[use])
+            return ref.at[:, pl.ds(*sp), pl.ds(*sr)], ref.at[:, pl.ds(*dp), pl.ds(*dr)]
+
+        return neighbours(make, k)
+
+    def side2(ref, use, count=1):
+        return sides(ref.at[:, own2, pl.ds(24, 16)], s["Z2"].at[:, pl.ds(use, count)])
 
     def merge2(ref, use):
-        for i in range(4):
-            p = 1 + 4 * gx + i
-            ref[0, p, 24:40, :] = (
-                ref[0, p, 24:40, :]
-                + turn(s["Z2"][use, 0, i], -32)
-                + turn(s["Z2"][use, 1, i], 32)
+        n = lane(16)
+        whole = [
+            ref[0, 1 + 4 * gx + i, 24:40, :]
+            + turn(s["Z2"][0, use, i], -32)
+            + turn(s["Z2"][1, use, i], 32)
+            for i in range(4)
+        ]
+        for i in range(2):
+            s["Q2"][use, gx, i, 16:32, :] = jnp.where(
+                n < 64, turn(whole[i], -32), turn(whole[i + 2], 32)
             )
 
-    def main2(ref):
+    def main2(use, count=1, first=None):
         copies = []
         for i in range(nx):
             for dy in (0, 1, -1):
                 if i == 0 and dy == 0:
                     continue
-                dr = {1: (8, 16), -1: (40, 16), 0: (24, 16)}[dy]
+                dr = {1: (0, 16), -1: (32, 16), 0: (16, 16)}[dy]
+                part = s["Q2"].at[pl.ds(use, count), gx]
                 copies.append(
                     links.copy(
-                        ref.at[0, own2, pl.ds(24, 16)],
-                        ref.at[0, own2, pl.ds(*dr)],
+                        part.at[:, :, pl.ds(16, 16)],
+                        part.at[:, :, pl.ds(*dr)],
                         (lax.rem(gx + i, nx), gy + dy, gz),
                         has["y", dy],
                         has["y", -dy],
+                        None if first is None else first + len(copies),
                     )
                 )
         return copies
 
-    def side3(use):
-        part = s["Z3"].at[use, gz]
+    def spread2(use, ref):
+        n = lane(48)
+        inside = (n >= 32) & (n < 96)
+        for g in range(nx):
+            for i in range(2):
+                v = s["Q2"][use, g, i]
+                ref[0, 1 + 4 * g + i, 8:56, :] = jnp.where(inside, turn(v, 32), 0.0)
+                ref[0, 3 + 4 * g + i, 8:56, :] = jnp.where(inside, turn(v, -32), 0.0)
+
+    def side3(use, count=1):
+        part = s["Z3"].at[gz, pl.ds(use, count)]
         return [links.copy(part, part, mate) for mate in line_mates]
 
     def merge3(ref, use):
         for i in range(2):
-            total = s["Z3"][use, 0, i]
+            total = s["Z3"][0, use, i]
             for q in range(1, nz):
-                total = total + s["Z3"][use, q, i]
+                total = total + s["Z3"][q, use, i]
             ref[0, 1 + 2 * gx + i, row3, :] = total
 
     def main3(ref):
-        part = ref.at[0, own3, row3]
+        part = ref.at[:, own3, row3]
         return [links.copy(part, part, mate) for mate in plane_mates]
 
     down1(s["K0"], 7, 16, s["K1"])
     down1(s["S0"], 7, 16, s["S1"])
-    sent = side1(s["K1"], 0) + side1(s["S1"], 1)
-    start(sent)
+    pack1(s["K1"], 0)
+    pack1(s["S1"], 1)
+    side_ks1 = side1(0, 2)
+    start(side_ks1)
     down2(s["K1"], s["K2"])
     down2(s["S1"], s["S2"])
-    more = side2(s["K2"], 0) + side2(s["S2"], 1)
-    start(more)
-    sent = sent + more
+    side_ks2 = side2(s["KS2"], 0, 2)
+    start(side_ks2)
     down3(s["K2"], 0)
     down3(s["S2"], 1)
-    more = side3(0) + side3(1)
-    start(more)
-    sent = sent + more
+    side_ks3 = side3(0, 2)
+    start(side_ks3)
 
     wait(side0)
     n64 = lane(64)
@@ -460,16 +486,15 @@
                 (n64 % 16) < 8, s["Z0"][0, a, g], s["Z0"][1, a, g]
             )
 
-    def ghost0(ref):
+    def ghost0(ref, k=None):
         def make(dx, dy):
             sg = {1: (2, 1), -1: (1, 1), 0: (1, 2)}[dx]
             dg = {1: (0, 1), -1: (3, 1), 0: (1, 2)}[dx]
             sr = {1: (64, 8), -1: (8, 8), 0: (8, 64)}[dy]
             dr = {1: (0, 8), -1: (72, 8), 0: (8, 64)}[dy]
-            every = slice(None)
-            return ref.at[every, pl.ds(*sg), pl.ds(*sr)], ref.at[every, pl.ds(*dg), pl.ds(*dr)]
-
-        return neighbours(make)
+            return ref.at[:, pl.ds(*sg), pl.ds(*sr)], ref.at[:, pl.ds(*dg), pl.ds(*dr)]
+
+        return neighbours(make, k)
 
     def unpack0(src, ref):
         n = lane(80)
@@ -485,16 +510,22 @@
     ghosts = ghost0(s["G0"])
     start(ghosts)
 
-    wait(sent)
+    wait(side_ks1)
     merge1(s["K1"], 0)
     merge1(s["S1"], 1)
+    main_ks1 = main1(s["KS1"], 7)
+    start(main_ks1)
+    wait(side_ks2)
     merge2(s["K2"], 0)
     merge2(s["S2"], 1)
+    first_main2 = links.used
+    main_ks2 = main2(0, 2)
+    start(main_ks2)
+    wait(side_ks3)
     merge3(s["K3"], 0)
     merge3(s["S3"], 1)
-    coarse = main1(s["K1"], 7) + main1(s["S1"], 7) + main2(s["K2"]) + main2(s["S2"])
-    coarse = coarse + main3(s["K3"]) + main3(s["S3"])
-    start(coarse)
+    main_ks3 = main3(s["KS3"])
+    start(main_ks3)
 
     wait(ghosts)
     for a, name in enumerate(("K0", "S0", "B0")):
@@ -507,9 +538,7 @@
 
     def finish0(t, p, r, n, diag, inverse):
         win = pl.ds(r, n)
-        scaled = b0[t, p, win, :] * inverse
-        b0[t, p, win, :] = scaled
-        xa0[t, p, win, :] = weights[0] * scaled
+        xa0[t, p, win, :] = inverse
         if t == 0:
             s["D0"][0, p, win, :] = diag
 
@@ -517,6 +546,17 @@
         return (8, 80, 16) if h > 4 else (12, 72, 24) if h > 0 else (16, 64, 16)
 
     level0.coefficients(s["K0"], s["S0"], c0, 1, 29, 4, 8, 80, 16, finish0)
+    wait(main_b)
+
+    def begin0(first, count):
+        for t in range(2):
+            for i in range(count):
+                part = (t, first + i, pl.ds(8, 80), slice(None))
+                scaled = b0[part] * xa0[part]
+                b0[part] = scaled
+                xa0[part] = weights[0] * scaled
+
+    groups(1, 29, 4, begin0)
     x, y = xa0, xb0
     for t in range(1, SWEEPS):
         h = 6 - t
@@ -526,10 +566,13 @@
     pre0 = x
 
     down1(s["R0"], 7, 16, s["B1"])
-    round1 = side1(s["B1"], 2)
+    pack1(s["B1"], 2)
+    round1 = side1(2)
     start(round1)
-
-    wait(coarse)
+    pack0(lambda i: pre0[0, 7 + i, 16:80, :], s["PN0"].at[0])
+    side_n0 = sides(s["PN0"], s["ZN0"])
+    start(side_n0)
+
     level1 = Level(1, 0.25)
     level2 = Level(1, 0.0625)
     level3 = Level(1, 0.015625, closed=True)
@@ -542,9 +585,6 @@
     def part2(h):
         return (1, 17, 16) + ((16, 32, 32) if h > 4 else (20, 24, 24))
 
-    down4(s["K3"], s["K4"])
-    down4(s["S3"], s["S4"])
-
     def finish(name):
         def keep(t, p, r, n, diag, inverse):
             s["D" + name][t, p, pl.ds(r, n), :] = diag
@@ -552,15 +592,30 @@
 
         return keep
 
+    wait(main_ks1)
     level1.coefficients(s["K1"], s["S1"], s["C1"], 2, 22, 5, 8, 48, 48, finish("1"))
     wait(round1)
     merge1(s["B1"], 2)
     round1 = main1(s["B1"], 6)
     start(round1)
 
-    pack0(lambda i: pre0[0, 7 + i, 16:80, :], s["PN0"].at[0])
-    side_n0 = sides(s["PN0"], s["ZN0"])
-    start(side_n0)
+    for i in range(16):
+        s["N0"][0, 7 + i, 16:80, :] = pre0[0, 7 + i, 16:80, :]
+    main_n0 = main0(s["N0"], 7, s["N0"], 6)
+    start(main_n0)
+    wait(side_n0)
+    for g in range(2):
+        s["GN0"][0, 1 + g, 8:72, :] = jnp.where(
+            (n64 % 16) < 8, s["ZN0"][0, 0, g], s["ZN0"][1, 0, g]
+        )
+    ghosts = ghost0(s["GN0"])
+    start(ghosts)
+    wait(main_ks2)
+    spread2(0, s["K2"])
+    spread2(1, s["S2"])
+    wait(main_ks3)
+    down4(s["K3"], s["K4"])
+    down4(s["S3"], s["S4"])
     level2.coefficients(s["K2"], s["S2"], s["C2"], 1, 17, 8, 16, 32, 32, finish("2"))
     level3.coefficients(s["K3"], s["S3"], s["C3"], *all3, finish("3"))
     level4.coefficients(s["K4"], s["S4"], s["C4"], *all4, finish("4"))
@@ -595,13 +650,19 @@
         s["N1"][0, 8 + i, 16:48, :] = jnp.where(
             (n32 >= 32) & (n32 < 96), x[0, 8 + i, 16:48, :], 0.0
         )
+    pack1(s["N1"], 3)
+    side_n1 = side1(3)
+    start(side_n1)
     wait(round2)
     merge2(s["B2"], 2)
-    round2 = main2(s["B2"])
+    round2 = main2(2)
     start(round2)
-    side_n1 = side1(s["N1"], 3)
-    start(side_n1)
+    wait(side_n1)
+    merge1(s["N1"], 3)
+    main_n1 = main1(s["N1"], 6, 0)
+    start(main_n1)
     wait(round2)
+    spread2(2, s["B2"])
     begin("2", *part2(6))
     x, y = s["XA2"], s["XB2"]
     for t in range(1, SWEEPS):
@@ -616,33 +677,17 @@
     for i in range(4):
         p = 1 + 4 * gx + i
         s["N2"][0, p, 24:40, :] = jnp.where((n16 >= 48) & (n16 < 80), x[0, p, 24:40, :], 0.0)
+    side_n2 = side2(s["N2"], 3)
+    start(side_n2)
     wait(round3)
     merge3(s["B3"], 2)
     round3 = main3(s["B3"])
     start(round3)
-
-    side_n2 = side2(s["N2"], 3)
-    start(side_n2)
-    wait(side_n0)
-    for g in range(2):
-        s["GN0"][0, 1 + g, 8:72, :] = jnp.where(
-            (n64 % 16) < 8, s["ZN0"][0, 0, g], s["ZN0"][1, 0, g]
-        )
-    ghosts = ghost0(s["GN0"])
-    wait(side_n1)
-    merge1(s["N1"], 3)
     wait(side_n2)
     merge2(s["N2"], 3)
     wait(round3)
-    main_n2 = main2(s["N2"])
+    main_n2 = main2(3, 1, first_main2)
     start(main_n2)
-    main_n1 = main1(s["N1"], 6)
-    start(main_n1)
-    start(ghosts)
-    for i in range(16):
-        s["N0"][0, 7 + i, 16:80, :] = pre0[0, 7 + i, 16:80, :]
-    main_n0 = main0(s["N0"], 7, s["N0"], 6)
-    start(main_n0)
 
     begin("3", *all3)
     x, y = s["XA3"], s["XB3"]
@@ -675,6 +720,7 @@
     e3 = y
 
     wait(main_n2)
+    spread2(3, s["N2"])
     rows3 = pl.ds(pl.multiple_of(8 * gy, 8), 24)
     spread(24, 8, doubling(16 * gz, 48, 16, 112), lambda i: e3[0, 1 + i, rows3, :], fine)
     y, x = s["XA2"], s["XB2"]
@@ -708,13 +754,14 @@
         s["E1"][0, 8 + i, 16:48, :] = jnp.where(
             (n32 >= 32) & (n32 < 96), y[0, 8 + i, 16:48, :], 0.0
         )
-    round1 = side1(s["E1"], 4)
+    pack1(s["E1"], 4)
+    round1 = side1(4)
     start(round1)
     wait(ghosts)
     unpack0(s["GN0"].at[0], s["N0"])
     wait(round1)
     merge1(s["E1"], 4)
-    round1 = main1(s["E1"], 3)
+    round1 = main1(s["E1"], 3, 8)
     start(round1)
     wait(main_n0)
     wait(round1)
@@ -756,13 +803,16 @@
     for level, dims in (("1", (24, 64, 128)), ("2", (18, 64, 128)), ("3", (10, 48, 128)), ("4", (6, 32, 128))):
         for name in ("K", "S", "B", "I", "D", "XA", "XB"):
             shapes[name + level] = (1,) + dims
+        if level != "4":
+            del shapes["K" + level], shapes["S" + level]
+            shapes["KS" + level] = (2,) + dims
         shapes["C" + level] = (6, 1) + dims
-    shapes["N1"] = shapes["E1"] = shapes["K1"]
-    shapes["N2"] = shapes["R2"] = shapes["K2"]
-    shapes["R3"] = shapes["K3"]
-    shapes["P1"], shapes["Z1"] = (5, 32, 128), (5, 2, 32, 128)
-    shapes["Z2"] = (4, 2, 4, 16, 128)
-    shapes["Z3"] = (3, 8, 2, 8, 128)
+    shapes["N1"] = shapes["E1"] = shapes["B1"]
+    shapes["N2"] = shapes["R2"] = shapes["B2"]
+    shapes["R3"] = shapes["B3"]
+    shapes["P1"], shapes["Z1"] = (5, 32, 128), (2, 5, 32, 128)
+    shapes["Z2"], shapes["Q2"] = (2, 4, 4, 16, 128), (4, 4, 2, 48, 128)
+    shapes["Z3"] = (8, 3, 2, 8, 128)
     shapes["T"], shapes["T1"] = (8, 56, 128), (24, 56, 128)
     return {
         "send": pltpu.SemaphoreType.DMA((COPIES,)),

time: 117 us -> 108 us (0.923)
  Pallas kernels: 115 us -> 106 us
    pallas_call x1, Pallas kernels: 115 us -> 106 us  [on_device(): pl.pallas_call(kernel, out_shape=jax.ShapeDtypeStruct(rhs.shape, F32), in...]
where the time goes in v3:
time: 108 us
  Pallas kernels  106 us (98%)
  local copies, waits for them, and re-layouts  1.89 us (2%)
    pallas_call x1, Pallas kernels, on_device(): pl.pallas_call(kernel, out_shape=jax.ShapeDtypeStruct(rhs.shape, F32), in...  106 us

profile of v3, /device:TPU:1, one launch (start us, length us, event | category | flops | bytes accessed | tf_op | source)
XLA Modules:
  0.0 107.7 jit_solution(11508548967564569799)
XLA Ops:
  0.0 105.8 %shard_map.37 = f32[16,64,128]{2,1,0:T(8,128)} custom-call(f32[16,64,128]{2,1,0:T(8,128)} %rhs.1, f32[16,64,128]{2,1,0:T(8,128)} %kappa.1, f32[16,64,128]{2,1,0:T(8,128)} %sigma.1), custom_call_target="tpu_custom_call" | custom-call | tf_op jit(solution)/shard_map/pallas_call | solution.py:826
  105.8 1.9 %copy.5 = f32[16,64,128]{2,1,0:T(8,128)} copy(f32[16,64,128]{2,1,0:T(8,128)} %shard_map.37) | data formatting | bytes 1048576

commit v4 on v3

--- a/solution.py
+++ b/solution.py
@@ -13,7 +13,7 @@
 BOTTOM_SWEEPS = 8
 MESH = pl.DeviceIdType.MESH
 F32 = jnp.float32
-COPIES = 148
+COPIES = 132
 
 
 def cheb(count):
@@ -333,7 +333,6 @@
     side0 = sides(s["P0"], s["Z0"])
     pl.semaphore_wait(barrier, len(plane_mates + line_mates))
     start(mains)
-    start(main_b)
     start(side0)
 
     to1 = halving(0, 32, 64)
@@ -507,25 +506,24 @@
                 if 0 <= p < 30:
                     ref[1, p, 8:88, :] = jnp.where(edge, turn(v, -16 * q - 8), 0.0)
 
+    first_ghost = links.used
     ghosts = ghost0(s["G0"])
     start(ghosts)
+    start(main_b)
 
     wait(side_ks1)
     merge1(s["K1"], 0)
     merge1(s["S1"], 1)
     main_ks1 = main1(s["KS1"], 7)
-    start(main_ks1)
     wait(side_ks2)
     merge2(s["K2"], 0)
     merge2(s["S2"], 1)
     first_main2 = links.used
     main_ks2 = main2(0, 2)
-    start(main_ks2)
     wait(side_ks3)
     merge3(s["K3"], 0)
     merge3(s["S3"], 1)
     main_ks3 = main3(s["KS3"])
-    start(main_ks3)
 
     wait(ghosts)
     for a, name in enumerate(("K0", "S0", "B0")):
@@ -547,6 +545,9 @@
 
     level0.coefficients(s["K0"], s["S0"], c0, 1, 29, 4, 8, 80, 16, finish0)
     wait(main_b)
+    start(main_ks1)
+    start(main_ks2)
+    start(main_ks3)
 
     def begin0(first, count):
         for t in range(2):
@@ -601,15 +602,13 @@
 
     for i in range(16):
         s["N0"][0, 7 + i, 16:80, :] = pre0[0, 7 + i, 16:80, :]
-    main_n0 = main0(s["N0"], 7, s["N0"], 6)
-    start(main_n0)
+    main_n0 = main0(s["N0"], 7, s["N0"], 6, 0)
     wait(side_n0)
     for g in range(2):
         s["GN0"][0, 1 + g, 8:72, :] = jnp.where(
             (n64 % 16) < 8, s["ZN0"][0, 0, g], s["ZN0"][1, 0, g]
         )
-    ghosts = ghost0(s["GN0"])
-    start(ghosts)
+    ghosts = ghost0(s["GN0"], first_ghost)
     wait(main_ks2)
     spread2(0, s["K2"])
     spread2(1, s["S2"])
@@ -634,6 +633,8 @@
         return cheb(BOTTOM_SWEEPS if name == "4" else SWEEPS)[0]
 
     wait(round1)
+    start(ghosts)
+    start(main_n0)
     begin("1", *part1(6))
     x, y = s["XA1"], s["XB1"]
     for t in range(1, SWEEPS):
@@ -659,9 +660,9 @@
     start(round2)
     wait(side_n1)
     merge1(s["N1"], 3)
-    main_n1 = main1(s["N1"], 6, 0)
+    main_n1 = main1(s["N1"], 6, 8)
+    wait(round2)
     start(main_n1)
-    wait(round2)
     spread2(2, s["B2"])
     begin("2", *part2(6))
     x, y = s["XA2"], s["XB2"]
@@ -761,7 +762,7 @@
     unpack0(s["GN0"].at[0], s["N0"])
     wait(round1)
     merge1(s["E1"], 4)
-    round1 = main1(s["E1"], 3, 8)
+    round1 = main1(s["E1"], 3, 16)
     start(round1)
     wait(main_n0)
     wait(round1)

time: 108 us -> 97.9 us (0.906)
  Pallas kernels: 106 us -> 95.8 us
    pallas_call x1, Pallas kernels: 106 us -> 95.8 us  [on_device(): pl.pallas_call(kernel, out_shape=jax.ShapeDtypeStruct(rhs.shape, F32), in...]
where the time goes in v4:
time: 97.9 us; the launch traced here: 97.7 us
  Pallas kernels  95.8 us (98%)
  local copies, waits for them, and re-layouts  1.89 us (2%)
    pallas_call x1, Pallas kernels, on_device(): pl.pallas_call(kernel, out_shape=jax.ShapeDtypeStruct(rhs.shape, F32), in...  95.8 us

profile of v4, /device:TPU:1, one launch (start us, length us, event | category | flops | bytes accessed | tf_op | source)
XLA Modules:
  0.0 97.7 jit_solution(285331209008602810)
XLA Ops:
  0.0 95.8 %shard_map.37 = f32[16,64,128]{2,1,0:T(8,128)} custom-call(f32[16,64,128]{2,1,0:T(8,128)} %rhs.1, f32[16,64,128]{2,1,0:T(8,128)} %kappa.1, f32[16,64,128]{2,1,0:T(8,128)} %sigma.1), custom_call_target="tpu_custom_call" | custom-call | tf_op jit(solution)/shard_map/pallas_call | solution.py:827
  95.8 1.9 %copy.5 = f32[16,64,128]{2,1,0:T(8,128)} copy(f32[16,64,128]{2,1,0:T(8,128)} %shard_map.37) | data formatting | bytes 1048576

commit v5 on v4

--- a/solution.py
+++ b/solution.py
@@ -669,9 +669,9 @@
     for t in range(1, SWEEPS):
         level2.sweep(x, y, s["B2"], s["C2"], weights[t], *part2(6 - t))
         x, y = y, x
-    level2.residual(x, s["B2"], s["C2"], s["D2"], s["R2"], 1, 17, 16, 24, 16, 16)
-
-    down3(s["R2"], 2)
+    level2.residual(x, s["B2"], s["C2"], s["D2"], y, 1, 17, 16, 24, 16, 16)
+
+    down3(y, 2)
     round3 = side3(2)
     start(round3)
     n16 = lane(16)
@@ -770,15 +770,18 @@
     to_main = doubling(32, 0, 0, 128)
     to_side = doubling(32, -128, 0, 8) + doubling(32, 128, 120, 128)
     xa0 = s["S0"]
-    for i in range(14):
-        e = s["E1"][0, 5 + i, 12:52, :]
+    for first in (0, 7):
+        coarse = jnp.concatenate([s["E1"][0, 5 + i, 12:52, :] for i in range(first, first + 7)], axis=0)
         for t, matrix in ((0, to_main), (1, to_side)):
-            part = product(e, matrix)
-            s["T0"][t, pl.ds(0, 40, stride=2), :] = part
-            s["T0"][t, pl.ds(1, 40, stride=2), :] = part
-            for o in range(2):
-                p = 1 + 2 * i + o
-                xa0[t, p, 8:88, :] = s["N0"][t, p, 8:88, :] + s["T0"][t, 0:80, :]
+            value = product(coarse, matrix)
+            for i in range(7):
+                part = value[40 * i : 40 * i + 40, :]
+                s["T0"][t, i, pl.ds(0, 40, stride=2), :] = part
+                s["T0"][t, i, pl.ds(1, 40, stride=2), :] = part
+        for i in range(7):
+            for t in range(2):
+                for p in (1 + 2 * (first + i), 2 + 2 * (first + i)):
+                    xa0[t, p, 8:88, :] = s["N0"][t, p, 8:88, :] + s["T0"][t, i, 0:80, :]
     x, y = s["XB0"], xa0
     for t in range(SWEEPS - 1):
         x, y = y, x
@@ -800,7 +803,7 @@
     shapes["P0"], shapes["Z0"], shapes["G0"] = (3, 2, 64, 128), (2, 3, 2, 64, 128), (3, 4, 80, 128)
     shapes["PN0"], shapes["ZN0"] = (1, 2, 64, 128), (2, 1, 2, 64, 128)
     shapes["GN0"] = (1, 4, 80, 128)
-    shapes["T0"] = (2, 88, 128)
+    shapes["T0"] = (2, 7, 88, 128)
     for level, dims in (("1", (24, 64, 128)), ("2", (18, 64, 128)), ("3", (10, 48, 128)), ("4", (6, 32, 128))):
         for name in ("K", "S", "B", "I", "D", "XA", "XB"):
             shapes[name + level] = (1,) + dims
@@ -809,7 +812,7 @@
             shapes["KS" + level] = (2,) + dims
         shapes["C" + level] = (6, 1) + dims
     shapes["N1"] = shapes["E1"] = shapes["B1"]
-    shapes["N2"] = shapes["R2"] = shapes["B2"]
+    shapes["N2"] = shapes["B2"]
     shapes["R3"] = shapes["B3"]
     shapes["P1"], shapes["Z1"] = (5, 32, 128), (2, 5, 32, 128)
     shapes["Z2"], shapes["Q2"] = (2, 4, 4, 16, 128), (4, 4, 2, 48, 128)

time: 97.9 us -> 97.3 us (level)
  no operation moved by 1% of the time
where the time goes in v5:
time: 97.3 us; the launch traced here: 97.2 us
  Pallas kernels  95.3 us (98%)
  local copies, waits for them, and re-layouts  1.89 us (2%)
    pallas_call x1, Pallas kernels, on_device(): pl.pallas_call(kernel, out_shape=jax.ShapeDtypeStruct(rhs.shape, F32), in...  95.3 us

profile of v5, /device:TPU:1, one launch (start us, length us, event | category | flops | bytes accessed | tf_op | source)
XLA Modules:
  0.0 97.2 jit_solution(5134134683785711056)
XLA Ops:
  0.0 95.3 %shard_map.37 = f32[16,64,128]{2,1,0:T(8,128)} custom-call(f32[16,64,128]{2,1,0:T(8,128)} %rhs.1, f32[16,64,128]{2,1,0:T(8,128)} %kappa.1, f32[16,64,128]{2,1,0:T(8,128)} %sigma.1), custom_call_target="tpu_custom_call" | custom-call | tf_op jit(solution)/shard_map/pallas_call | solution.py:830
  95.3 1.9 %copy.5 = f32[16,64,128]{2,1,0:T(8,128)} copy(f32[16,64,128]{2,1,0:T(8,128)} %shard_map.37) | data formatting | bytes 1048576
